TPU v7x, 512 devices: a whole 4x8x8 slice. The times are simulated.
512 devices in a mesh: dp: 32 (over z, x), block: 16 (over y, core).
Axes of the slice: x: 4, y: 8, z: 8, core: 2. Of those that a mesh axis runs over, the one named last changes fastest.
Arguments:
- gradient: float32 [1024, 16384], P('dp'), may hold values from -45 to 45
- left_root: float32 [16, 1024, 1024], P('block', 'dp'), may hold values from -0.1 to 4, as said below
- right_root: float32 [16, 1024, 1024], P('block', 'dp'), may hold values from -0.1 to 4, as said below
- first_moment: float32 [16, 1024, 1024], P('block', 'dp'), may hold values from -3 to 3
- second_moment: float32 [16, 1024, 1024], P('block', 'dp'), may hold values from 0.25 to 4
- step_count: int32 [1], replicated, may hold values from 1 to 40
- owner_table: int32 [16], replicated, may hold values from 0 to 15, each once
Outputs:
- update: float32 [1024, 16384], P('dp')
- first_new: float32 [16, 1024, 1024], P('block', 'dp')
- second_new: float32 [16, 1024, 1024], P('block', 'dp')
Inputs may be any that keep to these rules, and one draw needn't show every extreme that they name: `left_root`: symmetric in its last two dimensions. `right_root`: symmetric in its last two dimensions.
All inputs are finite; a program needn't handle non-finite values.
Results may differ from a plain program's by a relative error of at most 0.000086.
Values sent between devices are 32-bit elements; how exact they have to be, the bound alone decides.
No kernel may reach another device: no remote copies, remote signals or barrier semaphores. Data moves between devices by JAX's collectives and lax.ppermute only.
A program may use at most 64 MiB of HBM per device.

v0:
```python
import jax
import jax.numpy as jnp
from jax import lax
from jax.sharding import PartitionSpec as P

beta_one = 0.9
beta_two = 0.95
adam_eps = 1e-08
norm_eps = 1e-06


def local(gradient, left_root, right_root, first_moment, second_moment, step_count, owner_table):
    slot_count = left_root.shape[0]
    row_count = left_root.shape[1]
    block_width = left_root.shape[2]
    block_total = owner_table.shape[0]
    owner_index = lax.axis_index("block")
    positions = owner_index * slot_count + jnp.arange(slot_count, dtype=jnp.int32)
    matching = (owner_table[None, :] == positions[:, None]).astype(jnp.int32)
    chosen = jnp.sum(matching * jnp.arange(block_total, dtype=jnp.int32)[None, :], axis=1)
    grad_blocks = gradient.reshape(row_count, block_total, block_width)
    local_grad = jnp.transpose(jnp.take(grad_blocks, chosen, axis=1), (1, 0, 2))
    step_value = step_count[0].astype(jnp.float32)
    first_new = beta_one * first_moment + (1.0 - beta_one) * local_grad
    second_new = beta_two * second_moment + (1.0 - beta_two) * local_grad * local_grad
    first_fix = 1.0 - jnp.power(beta_one, step_value)
    second_fix = 1.0 - jnp.power(beta_two, step_value)
    adam_step = first_new / first_fix / (jnp.sqrt(second_new / second_fix) + adam_eps)
    adam_sq = jnp.sum(adam_step * adam_step, axis=(1, 2))
    adam_total = lax.psum(adam_sq, "dp")
    columns = local_grad
    right_side = jnp.einsum(
        "srk,skc->src",
        columns,
        lax.all_gather(right_root, "dp", axis=1, tiled=True),
        precision=lax.Precision.HIGHEST,
        preferred_element_type=jnp.float32,
    )
    columns = left_root
    precond = jnp.einsum(
        "srk,skc->src",
        columns,
        lax.all_gather(right_side, "dp", axis=1, tiled=True),
        precision=lax.Precision.HIGHEST,
        preferred_element_type=jnp.float32,
    )
    precond_sq = jnp.sum(precond * precond, axis=(1, 2))
    precond_total = lax.psum(precond_sq, "dp")
    graft_scale = jnp.sqrt(adam_total) / (jnp.sqrt(precond_total) + norm_eps)
    update_local = graft_scale[:, None, None] * precond
    flat_update = jnp.transpose(update_local, (1, 0, 2)).reshape(
        row_count, slot_count * block_width
    )
    gathered = lax.all_gather(flat_update, "block", axis=1, tiled=True)
    by_position = gathered.reshape(row_count, block_total, block_width)
    placed = jnp.take(by_position, owner_table, axis=1).reshape(
        row_count, block_total * block_width
    )
    return (placed, first_new, second_new)


def solution(mesh):
    in_specs = (
        P("dp", None),
        P("block", "dp", None),
        P("block", "dp", None),
        P("block", "dp", None),
        P("block", "dp", None),
        P(),
        P(),
    )
    out_specs = (P("dp", None), P("block", "dp", None), P("block", "dp", None))
    return jax.shard_map(local, mesh=mesh, in_specs=in_specs, out_specs=out_specs, check_vma=False)
```

profile of v0, /device:TPU:1, one launch (start us, length us, event | category | flops | bytes accessed | tf_op | source)
XLA Modules:
  0.0 327.3 jit_solution(9392277386682077936)
XLA Ops:
  7.2 0.0 copy-start
  7.2 0.0 all-gather.5.cloned.1.call-start
  7.2 0.7 all-gather.5.cloned.1.call-update
  7.9 0.0 all-gather.9.cloned.1.call-start
  8.0 1.3 compare_select_fusion
  11.9 0.0 copy-start.1
  11.9 0.0 copy-start.2
  12.0 2.9 copy.25
  14.8 0.0 copy-done.1
  14.8 0.0 copy-done.2
  14.8 1.5 multiply_reduce_fusion.1
  16.3 85.5 %all-gather.5.cloned.1.call-done = f32[1,1024,1024]{2,1,0:T(8,128)} async-done(((f32[1,32,1024]{2,1,0:T(8,128)}), f32[1,1024,1024]{2,1,0:T(8,128)}) %all-gather.5.cloned.1.call-update) | async-done | bytes 4194320 | tf_op jit(solution)/shard_map/all_gather | solution.py:35
  101.8 5.3 %fusion = f32[32,1024]{1,0:T(8,128)} fusion(f32[1,1024,1024]{2,1,0:T(8,128)} %all-gather.5.cloned.1.call-done, f32[32,1,1024]{2,1,0:T(1,128)S(1)} %get-tuple-element.25), kind=kOutput, calls=%fused_computation.1 | convolution fusion | flops 402653184 | bytes 4456448 | tf_op jit(solution)/shard_map/srk,skc->src/dot_general | solution.py:32
  107.2 0.0 all-gather.9.cloned.1.call-update
  107.2 0.0 copy-start.3
  107.2 0.0 all-gather.7.cloned.1.call-start
  107.2 84.9 %all-gather.9.cloned.1.call-done = f32[1024,1024]{1,0:T(8,128)} async-done(((f32[32,1024]{1,0:T(8,128)}), f32[1024,1024]{1,0:T(8,128)}) %all-gather.9.cloned.1.call-update) | async-done | bytes 4194320 | tf_op jit(solution)/shard_map/all_gather | solution.py:43
  192.1 0.0 copy-done
  192.1 5.3 %multiply_reduce_fusion = (f32[]{:T(128)}, f32[1024,32]{0,1:T(8,128)S(1)}) fusion(f32[1024,1024]{1,0:T(8,128)} %all-gather.9.cloned.1.call-done, f32[1,32,1024]{2,1,0:T(8,128)S(1)} %copy-done), kind=kOutput, calls=%fused_computation.17 | convolution fusion | flops 402718720 | bytes 4456452 | tf_op jit(solution)/shard_map/srk,skc->src/dot_general | solution.py:40
  197.4 58.6 %all-reduce = (f32[1]{0:T(128)}, f32[1]{0:T(128)}) all-reduce(f32[1]{0:T(128)} %bitcast.6, f32[1]{0:T(128)} %bitcast.9), channel_id=1, replica_groups=mesh['dp'=32,'block'=16] {'dp'}, use_global_device_ids=true, to_apply=%region_2.3 | all-reduce | flops 2 | bytes 16 | tf_op jit(solution)/shard_map/psum | solution.py:30
  257.5 0.7 multiply_bitcast_fusion
  258.1 0.0 all-gather.7.cloned.1.call-update
  258.2 0.0 copy-done.3
  258.2 0.1 broadcast_bitcast_fusion
  258.3 0.7 copy.19
  259.0 0.7 copy.20
  259.6 54.2 %all-gather.7.cloned.1.call-done = f32[32,16384]{1,0:T(8,128)} async-done(((f32[32,1024]{1,0:T(8,128)}), f32[32,16384]{1,0:T(8,128)}) %all-gather.7.cloned.1.call-update) | async-done | bytes 2097168 | tf_op jit(solution)/shard_map/all_gather | solution.py:54
  313.8 1.7 copy.39
  315.6 2.0 gather_fusion
  317.6 1.7 copy.23
  319.3 1.5 broadcast_select_fusion
  (3 shorter events, 0.0 us)
Async XLA Ops:
  7.2 184.9 %copy-start = (f32[1,32,1024]{2,1,0:T(8,128)S(1)}, f32[1,32,1024]{2,1,0:T(8,128)}, u32[]{:S(2)}) copy-start(f32[1,32,1024]{2,1,0:T(8,128)} %param.8) | copy-start | bytes 393220
  7.2 94.7 %all-gather.5.cloned.1.call-start = ((), (), s32[]{:S(2)}) async-start(), calls=%async_computation | async-start | bytes 4325376 | tf_op jit(solution)/shard_map/all_gather | solution.py:35
  7.9 184.2 %all-gather.9.cloned.1.call-start = ((), (), s32[]{:S(2)}) async-start(), calls=%async_computation.2 | async-start | bytes 4325376 | tf_op jit(solution)/shard_map/all_gather | solution.py:43
  11.9 2.9 copy-start.1
  11.9 2.9 copy-start.2
  107.2 151.0 %copy-start.3 = (s32[16]{0:T(128)S(1)}, s32[16]{0:T(128)}, u32[]{:S(2)}) copy-start(s32[16]{0:T(128)} %param.13) | copy-start | bytes 196
  107.2 206.6 %all-gather.7.cloned.1.call-start = ((), (), s32[]{:S(2)}) async-start(), calls=%async_computation.1 | async-start | bytes 2228224 | tf_op jit(solution)/shard_map/all_gather | solution.py:54
Sparse Core Ops, SparseCore 0:
  11.2 90.6 all-gather.4
  107.3 84.7 all-gather.8
  258.3 55.5 all-gather.6
where the time goes:
time: 328 us; the launch traced here: 327 us
  waiting for transfers between devices  225 us (69%)
  blocking collectives  58.6 us (18%)
  between operations  17.9 us (5%)
  matrix products  10.7 us (3%)
  local copies, waits for them, and re-layouts  9.78 us (3%)
  other arithmetic  4.95 us (2%)
    all_gather x1, waiting for transfers between devices, local(): lax.all_gather(right_root, 'dp', axis=1, tiled=True)  85.5 us
    all_gather x1, waiting for transfers between devices, local(): lax.all_gather(right_side, 'dp', axis=1, tiled=True)  84.9 us
    psum x1, blocking collectives, local(): adam_total = lax.psum(adam_sq, 'dp')  58.6 us
    all_gather x1, waiting for transfers between devices, local(): gathered = lax.all_gather(flat_update, 'block', axis=1, tiled=True)  54.2 us
  transfers between devices with their start and end apart: 3, of which 3 were waited for; matrix products, arithmetic and copies ran while one was open for 2% of the time, Pallas kernels for 0%

commit v1 on v0

v1 whole, which is shorter than its diff:
```python
import jax
import jax.numpy as jnp
from jax import lax
from jax.sharding import Mesh
from jax.sharding import PartitionSpec as P

beta_one = 0.9
beta_two = 0.95
adam_eps = 1e-08
norm_eps = 1e-06
HIGHEST = lax.Precision.HIGHEST


def gather_by_shifts(value, axis, count):
    me = lax.axis_index(axis)
    held = jnp.zeros((count,) + value.shape, value.dtype)
    for k in range(count):
        if k == 0:
            got = value
        else:
            got = lax.ppermute(value, axis, [(i, (i + k) % count) for i in range(count)])
        held = lax.dynamic_update_slice_in_dim(held, got[None], (me - k) % count, 0)
    return held


def gather_by_exchange(value, axes, count):
    return lax.all_to_all(
        jnp.broadcast_to(value[None], (count,) + value.shape), axes, 0, 0, tiled=True
    )


def local(gradient, left_root, right_root, first_moment, second_moment, step_count, owner_table):
    rows, width = left_root.shape[1], left_root.shape[2]
    blocks = owner_table.shape[0]
    quarters, near = lax.axis_size("q"), lax.axis_size("r") * lax.axis_size("x")
    ring = lax.axis_size("y")
    position = lax.axis_index("y") * 2 + lax.axis_index("core")
    chosen = jnp.sum(
        jnp.where(owner_table == position, jnp.arange(blocks, dtype=jnp.int32), 0)
    )
    grad = lax.dynamic_slice_in_dim(gradient, chosen * width, width, axis=1)

    grad_rows = gather_by_exchange(grad, ("r", "x"), near).reshape(near * rows, width)
    right_class = gather_by_shifts(right_root[0], "q", quarters).reshape(quarters * rows, width)

    step_value = step_count[0].astype(jnp.float32)
    first_new = beta_one * first_moment[0] + (1.0 - beta_one) * grad
    second_new = beta_two * second_moment[0] + (1.0 - beta_two) * grad * grad
    first_fix = 1.0 - jnp.power(beta_one, step_value)
    second_fix = 1.0 - jnp.power(beta_two, step_value)
    adam_step = first_new / first_fix / (jnp.sqrt(second_new / second_fix) + adam_eps)
    adam_sq = jnp.sum(adam_step * adam_step)

    right_side = lax.dot_general(
        grad_rows, right_class, (((1,), (1,)), ((), ())), precision=HIGHEST
    )
    left_rows = gather_by_exchange(left_root[0], ("r", "x"), near).reshape(near * rows, width)
    right_all = gather_by_shifts(right_side, "q", quarters).reshape(width, quarters * rows)
    precond = jnp.dot(left_rows, right_all, precision=HIGHEST)

    sums = jnp.stack([adam_sq, jnp.sum(precond * precond)])
    pieces = precond.reshape(near, rows, quarters * rows)
    tail = jnp.broadcast_to(
        jnp.pad(sums, (0, quarters * rows - 2))[None, None, :], (near, 8, quarters * rows)
    )
    sent = jnp.concatenate([pieces, tail], axis=1)
    got = lax.all_to_all(sent, ("r", "x"), 0, 0, tiled=True)
    mine = got[:, :rows].reshape(near, rows, quarters, rows)
    mine = jnp.transpose(mine, (1, 2, 0, 3)).reshape(rows, width)
    near_sums = jnp.sum(got[:, rows, :2], axis=0)

    own = gather_by_exchange(mine, "y", ring)
    totals = jnp.sum(lax.all_gather(near_sums, "q"), axis=0)
    scale = jnp.sqrt(totals[0]) / (jnp.sqrt(totals[1]) + norm_eps)
    scales = lax.all_gather(scale, ("y", "core"))
    other = lax.ppermute(own, "core", [(0, 1), (1, 0)])
    core = lax.axis_index("core")
    even = jnp.where(core == 0, own, other)
    odd = jnp.where(core == 0, other, own)
    both = jnp.stack([even, odd], axis=1).reshape(blocks, rows, width)
    placed = jnp.take(both, owner_table, axis=0) * jnp.take(scales, owner_table)[:, None, None]
    update = jnp.transpose(placed, (1, 0, 2)).reshape(rows, blocks * width)
    return update, first_new[None], second_new[None]


def solution(mesh):
    fine = Mesh(mesh.devices.reshape(4, 2, 4, 8, 2), ("q", "r", "x", "y", "core"))
    near, deep = ("q", "r", "x"), ("y", "core")
    flat, owned = P(near, None), P(deep, near, None)
    return jax.shard_map(
        local,
        mesh=fine,
        in_specs=(flat, owned, owned, owned, owned, P(), P()),
        out_specs=(flat, owned, owned),
        check_vma=False,
    )
```

time: 328 us -> 162 us (0.49)
  waiting for transfers between devices: 225 us -> 13.4 us
  starting transfers between devices: 0.12 us -> 49.5 us
  blocking collectives: 58.6 us -> 73.7 us
  between operations: 17.9 us -> 3.07 us
  matrix products: 10.7 us -> 2.59 us
  other arithmetic: 4.95 us -> 8.53 us
    all_gather x3 -> x0, waiting for transfers between devices: 225 us -> none  [the longest x1 85.5 us: local(): lax.all_gather(right_root, 'dp', axis=1, tiled=True)]
    psum x1 -> x0, blocking collectives: 58.6 us -> none  [local(): adam_total = lax.psum(adam_sq, 'dp')]
    all_to_all x0 -> x2, blocking collectives: none -> 38.7 us  [the longest x1 29.6 us: gather_by_exchange(): lax.all_to_all(jnp.broadcast_to(value[None], (count,) + value.shape), axe...]
    ppermute x0 -> x7, starting transfers between devices: none -> 37.7 us  [the longest x6 29.1 us: gather_by_shifts(): lax.ppermute(value, axis, [(i, (i + k) % count) for i in range(count)])]
    unnamed x0 -> x2, blocking collectives: none -> 35 us
    ppermute x0 -> x7, waiting for transfers between devices: none -> 13.4 us  [the longest x6 13.4 us: gather_by_shifts(): lax.ppermute(value, axis, [(i, (i + k) % count) for i in range(count)])]
    all_to_all x0 -> x2, starting transfers between devices: none -> 11.8 us  [gather_by_exchange(): lax.all_to_all(jnp.broadcast_to(value[None], (count,) + value.shape), axe...]
    dot_general x2, matrix products: 10.7 us -> 2.59 us  [the longest x1 1.61 us: local(): precond = jnp.dot(left_rows, right_all, precision=HIGHEST)]
  transfers between devices with their start and end apart: 3 -> 9, of which waited for: 3 -> 4; matrix products, arithmetic and copies ran while one was open for 2% -> 5% of each run, Pallas kernels for 0% -> 0%
where the time goes in v1:
time: 162 us; the launch traced here: 161 us
  blocking collectives  73.7 us (45%)
  starting transfers between devices  49.5 us (31%)
  waiting for transfers between devices  13.4 us (8%)
  local copies, waits for them, and re-layouts  10.6 us (7%)
  other arithmetic  8.53 us (5%)
  between operations  3.07 us (2%)
  matrix products  2.59 us (2%)
    unnamed x2, blocking collectives  35 us
    all_to_all x1, blocking collectives, gather_by_exchange(): lax.all_to_all(jnp.broadcast_to(value[None], (count,) + value.shape), axe...  29.6 us
    ppermute x6, starting transfers between devices, gather_by_shifts(): lax.ppermute(value, axis, [(i, (i + k) % count) for i in range(count)])  29.1 us
    ppermute x6, waiting for transfers between devices, gather_by_shifts(): lax.ppermute(value, axis, [(i, (i + k) % count) for i in range(count)])  13.4 us
    all_to_all x2, starting transfers between devices, gather_by_exchange(): lax.all_to_all(jnp.broadcast_to(value[None], (count,) + value.shape), axe...  11.8 us
    all_to_all x1, blocking collectives, local(): got = lax.all_to_all(sent, ('r', 'x'), 0, 0, tiled=True)  9.15 us
    ppermute x1, starting transfers between devices, local(): other = lax.ppermute(own, 'core', [(0, 1), (1, 0)])  8.6 us
  transfers between devices with their start and end apart: 9, of which 4 were waited for; matrix products, arithmetic and copies ran while one was open for 5% of the time, Pallas kernels for 0%

profile of v1, /device:TPU:1, one launch (start us, length us, event | category | flops | bytes accessed | tf_op | source)
XLA Modules:
  0.0 161.5 jit_solution(11519922516253450327)
XLA Ops:
  0.6 1.3 compare_select_fusion
  2.6 1.7 %fusion.2 = (f32[1,32,1024]{2,1,0:T(8,128)}, f32[32,1024]{1,0:T(8,128)S(1)}) fusion(f32[1,32,1024]{2,1,0:T(8,128)} %param.11, f32[32,16384]{1,0:T(8,128)} %param.7, s32[]{:T(128)S(6)} %select_n.84), kind=kLoop, calls=%fused_computation.22 | loop fusion | flops 131072 | bytes 524292 | tf_op jit(solution)/shard_map/broadcast_in_dim | solution.py:83
  4.3 1.1 broadcast_in_dim.78
  5.4 6.7 %all-to-all-start = ((f32[8,32,1024]{2,1,0:T(8,128)}), f32[8,32,1024]{2,1,0:T(8,128)S(1)}, u32[]{:S(2)}, u32[]{:S(2)}) async-start(f32[8,32,1024]{2,1,0:T(8,128)} %broadcast_in_dim.78), calls=%async_computation | async-start | bytes 2097152 | tf_op jit(solution)/shard_map/all_to_all | solution.py:27
  12.0 5.8 %collective-permute-start = (f32[32,1024]{1,0:T(8,128)S(1)}, f32[32,1024]{1,0:T(8,128)S(1)}, u32[]{:S(2)}, u32[]{:S(2)}) collective-permute-start(f32[32,1024]{1,0:T(8,128)S(1)} %bitcast.74), channel_id=1, source_target_pairs={{0,128},{128,256},{256,384},{384,0},{1,129},{129,257},{257,385},{3... | collective-permute-start | bytes 393224 | tf_op jit(solution)/shard_map/ppermute | solution.py:21
  17.9 5.9 %collective-permute-start.2 = (f32[32,1024]{1,0:T(8,128)S(1)}, f32[32,1024]{1,0:T(8,128)S(1)}, u32[]{:S(2)}, u32[]{:S(2)}) collective-permute-start(f32[32,1024]{1,0:T(8,128)S(1)} %bitcast.75), channel_id=1, source_target_pairs={{0,384},{128,0},{256,128},{384,256},{1,385},{129,1},{257,129},{385... | collective-permute-start | bytes 393224 | tf_op jit(solution)/shard_map/ppermute | solution.py:21
  23.7 5.5 %collective-permute-start.1 = (f32[32,1024]{1,0:T(8,128)S(1)}, f32[32,1024]{1,0:T(8,128)S(1)}, u32[]{:S(2)}, u32[]{:S(2)}) collective-permute-start(f32[32,1024]{1,0:T(8,128)S(1)} %bitcast.76), channel_id=1, source_target_pairs={{0,256},{128,384},{256,0},{384,128},{1,257},{129,385},{257,1},{385... | collective-permute-start | bytes 393224 | tf_op jit(solution)/shard_map/ppermute | solution.py:21
  30.1 0.0 all-to-all-done
  30.1 1.1 broadcast_in_dim.88
  31.2 5.1 %all-to-all-start.1 = ((f32[8,32,1024]{2,1,0:T(8,128)}), f32[8,32,1024]{2,1,0:T(8,128)S(1)}, u32[]{:S(2)}, u32[]{:S(2)}) async-start(f32[8,32,1024]{2,1,0:T(8,128)} %broadcast_in_dim.88), calls=%async_computation.1 | async-start | bytes 2097152 | tf_op jit(solution)/shard_map/all_to_all | solution.py:27
  36.3 0.0 copy-start.2
  36.3 0.7 collective-permute-done
  37.1 3.8 %collective-permute-done.1 = f32[32,1024]{1,0:T(8,128)S(1)} collective-permute-done((f32[32,1024]{1,0:T(8,128)S(1)}, f32[32,1024]{1,0:T(8,128)S(1)}, u32[]{:S(2)}, u32[]{:S(2)}) %collective-permute-start.1) | collective-permute-done | bytes 131104 | tf_op jit(solution)/shard_map/ppermute | solution.py:21
  40.9 0.0 collective-permute-done.2
  41.0 1.0 bitcast_dynamic-update-slice_fusion.3
  42.0 4.9 %collective-permute-start.3 = (f32[256,128]{1,0:T(8,128)S(1)}, f32[256,128]{1,0:T(8,128)S(1)}, u32[]{:S(2)}, u32[]{:S(2)}) collective-permute-start(f32[256,128]{1,0:T(8,128)S(1)} %get-tuple-element.14), channel_id=1, source_target_pairs={{0,128},{128,256},{256,384},{384,0},{1,129},{129,257},{257,385},{3... | collective-permute-start | bytes 393224 | tf_op jit(solution)/shard_map/ppermute | solution.py:21
  46.9 1.3 fusion.1
  48.3 2.1 %collective-permute-start.4 = (f32[256,128]{1,0:T(8,128)S(1)}, f32[256,128]{1,0:T(8,128)S(1)}, u32[]{:S(2)}, u32[]{:S(2)}) collective-permute-start(f32[256,128]{1,0:T(8,128)S(1)} %get-tuple-element.14), channel_id=1, source_target_pairs={{0,256},{128,384},{256,0},{384,128},{1,257},{129,385},{257,1},{385... | collective-permute-start | bytes 393224 | tf_op jit(solution)/shard_map/ppermute | solution.py:21
  50.4 5.0 %collective-permute-start.5 = (f32[256,128]{1,0:T(8,128)S(1)}, f32[256,128]{1,0:T(8,128)S(1)}, u32[]{:S(2)}, u32[]{:S(2)}) collective-permute-start(f32[256,128]{1,0:T(8,128)S(1)} %get-tuple-element.14), channel_id=1, source_target_pairs={{0,384},{128,0},{256,128},{384,256},{1,385},{129,1},{257,129},{385... | collective-permute-start | bytes 393224 | tf_op jit(solution)/shard_map/ppermute | solution.py:21
  55.4 0.5 collective-permute-done.3
  55.9 8.4 %collective-permute-done.4 = f32[256,128]{1,0:T(8,128)S(1)} collective-permute-done((f32[256,128]{1,0:T(8,128)S(1)}, f32[256,128]{1,0:T(8,128)S(1)}, u32[]{:S(2)}, u32[]{:S(2)}) %collective-permute-start.4) | collective-permute-done | bytes 131104 | tf_op jit(solution)/shard_map/ppermute | solution.py:21
  64.3 0.0 collective-permute-done.5
  64.3 0.0 all-to-all-done.1
  64.3 1.6 multiply_reduce_fusion
  65.9 0.1 copy.13
  66.0 1.3 fusion.3
  67.4 9.1 %all_to_all.20 = f32[8,40,128]{2,1,0:T(8,128)S(1)} all-to-all(f32[8,40,128]{2,1,0:T(8,128)S(1)} %pad_maximum_fusion.1), channel_id=1, replica_groups=mesh['q'=4,'r'=2,'x'=4,'y'=8,'core'=2] {'r','x'}, dimensions={0} | all-to-all | bytes 327680 | tf_op jit(solution)/shard_map/all_to_all | solution.py:67
  76.5 0.3 reshape.67
  76.8 0.3 copy.19
  77.1 0.0 copy-start.4
  77.1 0.2 broadcast_in_dim.90
  77.4 0.1 broadcast_in_dim.91
  77.5 29.6 %all_to_all.21 = f32[8,32,1024]{2,1,0:T(8,128)S(1)} all-to-all(f32[8,32,1024]{2,1,0:T(8,128)S(1)} %broadcast_in_dim.91), channel_id=1, replica_groups=mesh['q'=4,'r'=2,'x'=4,'y'=8,'core'=2] {'y'}, dimensions={0} | all-to-all | bytes 2097152 | tf_op jit(solution)/shard_map/all_to_all | solution.py:27
  107.1 8.6 %collective-permute-start.6 = (f32[8,32,1024]{2,1,0:T(8,128)S(1)}, f32[8,32,1024]{2,1,0:T(8,128)S(1)}, u32[]{:S(2)}, u32[]{:S(2)}) collective-permute-start(f32[8,32,1024]{2,1,0:T(8,128)S(1)} %all_to_all.21), channel_id=1, source_target_pairs={{0,1},{1,0},{2,3},{3,2},{4,5},{5,4},{6,7},{7,6},{8,9},{9,8},{10,11... | collective-permute-start | bytes 3145736 | tf_op jit(solution)/shard_map/ppermute | solution.py:76
  115.7 1.3 dynamic-slice
  117.7 0.2 dynamic-update-slice
  117.9 1.3 dynamic-slice.1
  119.2 10.3 %all-reduce.1 = f32[8]{0:T(128)S(1)} all-reduce(f32[8]{0:T(128)S(1)} %dynamic-update-slice), channel_id=2, replica_groups=mesh['q'=4,'r'=2,'x'=4,'y'=8,'core'=2] {'q'}, use_global_device_ids=true, to_apply=%add.1 | all-reduce | flops 8 | bytes 64
  129.5 0.1 reshape.86
  129.6 0.8 divide_dynamic-update-slice_fusion
  130.5 24.6 %all-reduce.2 = f32[16]{0:T(128)S(1)} all-reduce(f32[16]{0:T(128)S(1)} %divide_dynamic-update-slice_fusion), channel_id=1, replica_groups=mesh['q'=4,'r'=2,'x'=4,'y'=8,'core'=2] {'y','core'}, use_global_device_ids=true, to_apply=%add.2 | all-reduce | flops 16 | bytes 128
  155.1 0.7 gather_fusion.1
  155.8 0.0 collective-permute-done.6
  155.8 0.2 select_bitcast_fusion.1
  156.0 1.5 pad_maximum_fusion
  157.4 2.3 %gather_fusion = f32[16,32,1024]{2,1,0:T(8,128)S(1)} fusion(f32[16,32,1024]{2,1,0:T(8,128)} %bitcast.65, s32[1024]{0:T(1024)S(1)} %pad_clamp_fusion), kind=kCustom, calls=%fused_computation | custom fusion | bytes 4194368 | tf_op jit(solution)/shard_map/jit(_take)/gather | solution.py:81
  159.7 0.3 multiply_bitcast_fusion
  160.0 1.5 copy.17
  (26 shorter events, 0.3 us)
Async XLA Ops:
  0.6 11.4 %copy-start.3 = (f32[1,32,1024]{2,1,0:T(8,128)S(1)}, f32[1,32,1024]{2,1,0:T(8,128)}, u32[]{:S(2)}) copy-start(f32[1,32,1024]{2,1,0:T(8,128)} %param.9) | copy-start | bytes 393220
  4.3 25.8 %copy-start.1 = (f32[1,32,1024]{2,1,0:T(8,128)S(1)}, f32[1,32,1024]{2,1,0:T(8,128)}, u32[]{:S(2)}) copy-start(f32[1,32,1024]{2,1,0:T(8,128)} %param.8) | copy-start | bytes 393220
  5.4 24.7 %all-to-all-start = ((f32[8,32,1024]{2,1,0:T(8,128)}), f32[8,32,1024]{2,1,0:T(8,128)S(1)}, u32[]{:S(2)}, u32[]{:S(2)}) async-start(f32[8,32,1024]{2,1,0:T(8,128)} %broadcast_in_dim.78), calls=%async_computation | async-start | bytes 2097152 | tf_op jit(solution)/shard_map/all_to_all | solution.py:27
  12.0 25.0 %collective-permute-start = (f32[32,1024]{1,0:T(8,128)S(1)}, f32[32,1024]{1,0:T(8,128)S(1)}, u32[]{:S(2)}, u32[]{:S(2)}) collective-permute-start(f32[32,1024]{1,0:T(8,128)S(1)} %bitcast.74), channel_id=1, source_target_pairs={{0,128},{128,256},{256,384},{384,0},{1,129},{129,257},{257,385},{3... | collective-permute-start | bytes 393224 | tf_op jit(solution)/shard_map/ppermute | solution.py:21
  17.9 23.1 %collective-permute-start.2 = (f32[32,1024]{1,0:T(8,128)S(1)}, f32[32,1024]{1,0:T(8,128)S(1)}, u32[]{:S(2)}, u32[]{:S(2)}) collective-permute-start(f32[32,1024]{1,0:T(8,128)S(1)} %bitcast.75), channel_id=1, source_target_pairs={{0,384},{128,0},{256,128},{384,256},{1,385},{129,1},{257,129},{385... | collective-permute-start | bytes 393224 | tf_op jit(solution)/shard_map/ppermute | solution.py:21
  23.7 17.2 %collective-permute-start.1 = (f32[32,1024]{1,0:T(8,128)S(1)}, f32[32,1024]{1,0:T(8,128)S(1)}, u32[]{:S(2)}, u32[]{:S(2)}) collective-permute-start(f32[32,1024]{1,0:T(8,128)S(1)} %bitcast.76), channel_id=1, source_target_pairs={{0,256},{128,384},{256,0},{384,128},{1,257},{129,385},{257,1},{385... | collective-permute-start | bytes 393224 | tf_op jit(solution)/shard_map/ppermute | solution.py:21
  31.2 33.1 %all-to-all-start.1 = ((f32[8,32,1024]{2,1,0:T(8,128)}), f32[8,32,1024]{2,1,0:T(8,128)S(1)}, u32[]{:S(2)}, u32[]{:S(2)}) async-start(f32[8,32,1024]{2,1,0:T(8,128)} %broadcast_in_dim.88), calls=%async_computation.1 | async-start | bytes 2097152 | tf_op jit(solution)/shard_map/all_to_all | solution.py:27
  36.3 10.6 %copy-start = (f32[1,32,1024]{2,1,0:T(8,128)S(1)}, f32[1,32,1024]{2,1,0:T(8,128)}, u32[]{:S(2)}) copy-start(f32[1,32,1024]{2,1,0:T(8,128)} %param.11) | copy-start | bytes 393220
  36.3 10.6 %copy-start.2 = (f32[1,32,1024]{2,1,0:T(8,128)S(1)}, f32[1,32,1024]{2,1,0:T(8,128)}, u32[]{:S(2)}) copy-start(f32[1,32,1024]{2,1,0:T(8,128)} %param.10) | copy-start | bytes 393220
  42.0 13.9 %collective-permute-start.3 = (f32[256,128]{1,0:T(8,128)S(1)}, f32[256,128]{1,0:T(8,128)S(1)}, u32[]{:S(2)}, u32[]{:S(2)}) collective-permute-start(f32[256,128]{1,0:T(8,128)S(1)} %get-tuple-element.14), channel_id=1, source_target_pairs={{0,128},{128,256},{256,384},{384,0},{1,129},{129,257},{257,385},{3... | collective-permute-start | bytes 393224 | tf_op jit(solution)/shard_map/ppermute | solution.py:21
  48.3 16.0 %collective-permute-start.4 = (f32[256,128]{1,0:T(8,128)S(1)}, f32[256,128]{1,0:T(8,128)S(1)}, u32[]{:S(2)}, u32[]{:S(2)}) collective-permute-start(f32[256,128]{1,0:T(8,128)S(1)} %get-tuple-element.14), channel_id=1, source_target_pairs={{0,256},{128,384},{256,0},{384,128},{1,257},{129,385},{257,1},{385... | collective-permute-start | bytes 393224 | tf_op jit(solution)/shard_map/ppermute | solution.py:21
  50.4 13.9 %collective-permute-start.5 = (f32[256,128]{1,0:T(8,128)S(1)}, f32[256,128]{1,0:T(8,128)S(1)}, u32[]{:S(2)}, u32[]{:S(2)}) collective-permute-start(f32[256,128]{1,0:T(8,128)S(1)} %get-tuple-element.14), channel_id=1, source_target_pairs={{0,384},{128,0},{256,128},{384,256},{1,385},{129,1},{257,129},{385... | collective-permute-start | bytes 393224 | tf_op jit(solution)/shard_map/ppermute | solution.py:21
  77.1 78.6 %copy-start.4 = (s32[16]{0:T(128)S(1)}, s32[16]{0:T(128)}, u32[]{:S(2)}) copy-start(s32[16]{0:T(128)} %param.13) | copy-start | bytes 196
  107.1 48.7 %collective-permute-start.6 = (f32[8,32,1024]{2,1,0:T(8,128)S(1)}, f32[8,32,1024]{2,1,0:T(8,128)S(1)}, u32[]{:S(2)}, u32[]{:S(2)}) collective-permute-start(f32[8,32,1024]{2,1,0:T(8,128)S(1)} %all_to_all.21), channel_id=1, source_target_pairs={{0,1},{1,0},{2,3},{3,2},{4,5},{5,4},{6,7},{7,6},{8,9},{9,8},{10,11... | collective-permute-start | bytes 3145736 | tf_op jit(solution)/shard_map/ppermute | solution.py:76

commit v2 on v1

v2 whole, which is shorter than its diff:
```python
import functools

import jax
import jax.numpy as jnp
from jax import lax
from jax.experimental import pallas as pl
from jax.experimental.pallas import tpu as pltpu
from jax.sharding import Mesh
from jax.sharding import PartitionSpec as P

beta_one = 0.9
beta_two = 0.95
adam_eps = 1e-08
norm_eps = 1e-06
HIGHEST = lax.Precision.HIGHEST
GROUP = 4


def exchange(value, axes):
    return lax.all_to_all(value, axes, 0, 0, tiled=True)


def copies(value, count):
    return jnp.broadcast_to(value[None], (count,) + value.shape)


def place_kernel(spread, ring, rows, table, core, sums, own, other, out, scale):
    step = pl.program_id(0)

    @pl.when(step == 0)
    def _():
        total = jnp.sum(sums[...], axis=0)
        factor = jnp.sqrt(total[:, :, 0:1]) / (jnp.sqrt(total[:, :, 1:2]) + norm_eps)
        scale[...] = jnp.broadcast_to(factor.reshape(2 * ring, 1), scale.shape)

    lane = lax.broadcasted_iota(jnp.int32, (rows, 128), 1) // rows
    for k in range(GROUP):
        position = table[step * GROUP + k]
        deep = position // 2
        part = position - 2 * deep
        mine = part == core[0]
        factor = scale[pl.ds(part * ring + deep, 1), :]
        pieces = []
        for x in range(spread):
            held = own[x, deep, : 2 * rows, :]
            got = other[x, deep, : 2 * rows, :]
            pieces.append(jnp.where(mine, held, got) * factor)
        for z in range(ring):
            half, slot = z // 4, z % 4
            tile = jnp.zeros((rows, 128), jnp.float32)
            for x in range(spread):
                part_x = pieces[x][half * rows : (half + 1) * rows, :]
                if x != slot:
                    part_x = pltpu.roll(part_x, (x - slot) % 4 * rows, 1)
                tile = jnp.where(lane == x, part_x, tile)
            out[:, pl.ds(k * 1024 + z * 128, 128)] = tile


def place(table, core, sums, own, other, spread, ring, rows):
    blocks = table.shape[0]
    return pl.pallas_call(
        functools.partial(place_kernel, spread, ring, rows),
        out_shape=jax.ShapeDtypeStruct((rows, blocks * 1024), jnp.float32),
        grid_spec=pltpu.PrefetchScalarGridSpec(
            num_scalar_prefetch=2,
            grid=(blocks // GROUP,),
            in_specs=[
                pl.BlockSpec(sums.shape, lambda i, *_: (0, 0, 0, 0)),
                pl.BlockSpec(own.shape, lambda i, *_: (0, 0, 0, 0)),
                pl.BlockSpec(other.shape, lambda i, *_: (0, 0, 0, 0)),
            ],
            out_specs=pl.BlockSpec((rows, GROUP * 1024), lambda i, *_: (0, i)),
            scratch_shapes=[pltpu.VMEM((blocks, 128), jnp.float32)],
        ),
        compiler_params=pltpu.CompilerParams(vmem_limit_bytes=32 * 1024 * 1024),
        name="place",
    )(table, core, sums, own, other)


def local(gradient, left_root, right_root, first_moment, second_moment, step_count, owner_table):
    rows, width = left_root.shape[1], left_root.shape[2]
    blocks = owner_table.shape[0]
    deep, spread, ring = lax.axis_size("z"), lax.axis_size("x"), lax.axis_size("y")
    core = lax.axis_index("core")
    position = lax.axis_index("y") * 2 + core

    right_class = exchange(copies(right_root[0], deep), "z").reshape(deep * rows, width)

    chosen = jnp.sum(
        jnp.where(owner_table == position, jnp.arange(blocks, dtype=jnp.int32), 0)
    )
    grad = lax.dynamic_slice_in_dim(gradient, chosen * width, width, axis=1)
    grad_rows = lax.all_gather(grad, "x", axis=0, tiled=True)

    step_value = step_count[0].astype(jnp.float32)
    first_new = beta_one * first_moment[0] + (1.0 - beta_one) * grad
    second_new = beta_two * second_moment[0] + (1.0 - beta_two) * grad * grad
    first_fix = 1.0 - jnp.power(beta_one, step_value)
    second_fix = 1.0 - jnp.power(beta_two, step_value)
    adam_step = first_new / first_fix / (jnp.sqrt(second_new / second_fix) + adam_eps)
    adam_sq = jnp.sum(adam_step * adam_step)

    right_side = lax.dot_general(
        grad_rows, right_class, (((1,), (1,)), ((), ())), precision=HIGHEST
    )
    left_own, right_side = lax.optimization_barrier((left_root[0], right_side))
    left_rows = lax.all_gather(left_own, "x", axis=0, tiled=True)
    right_all = exchange(copies(right_side, deep), "z").reshape(width, deep * rows)
    precond = jnp.dot(left_rows, right_all, precision=HIGHEST)

    sums = jnp.stack([adam_sq, jnp.sum(precond * precond)])
    tail = jnp.broadcast_to(jnp.pad(sums, (0, 126))[None, None, :], (spread, 8, 128))
    pieces = jnp.transpose(precond.reshape(spread, rows, 2, 128), (0, 2, 1, 3))
    sent = jnp.concatenate([pieces.reshape(spread, 2 * rows, 128), tail], axis=1)
    sent = jnp.broadcast_to(sent[:, None], (spread, ring) + sent.shape[1:])
    own = exchange(sent.reshape(spread * ring, 2 * rows + 8, 128), ("x", "y"))
    other = lax.ppermute(own, "core", [(0, 1), (1, 0)])
    own = own.reshape(spread, ring, 2 * rows + 8, 128)
    other = other.reshape(spread, ring, 2 * rows + 8, 128)
    near = jnp.sum(own[:, :, 2 * rows, :], axis=0)
    totals = exchange(copies(near, deep * 2), ("z", "core")).reshape(deep, 2, ring, 128)
    update = place(
        owner_table, core.astype(jnp.int32)[None], totals, own, other, spread, ring, rows
    )
    return update, first_new[None], second_new[None]


def solution(mesh):
    fine = Mesh(mesh.devices.reshape(8, 4, 8, 2), ("z", "x", "y", "core"))
    near, deep = ("z", "x"), ("y", "core")
    flat, owned = P(near, None), P(deep, near, None)
    return jax.shard_map(
        local,
        mesh=fine,
        in_specs=(flat, owned, owned, owned, owned, P(), P()),
        out_specs=(flat, owned, owned),
        check_vma=False,
    )
```

time: 162 us -> 140 us (0.86)
  starting transfers between devices: 49.5 us -> 18.9 us
  waiting for transfers between devices: 13.4 us -> 30.3 us
  local copies, waits for them, and re-layouts: 10.6 us -> 3.24 us
  Pallas kernels: 0 us -> 3.76 us
  other arithmetic: 8.53 us -> 4.96 us
    unnamed x2 -> x0, blocking collectives: 35 us -> none
    all_to_all x2, waiting for transfers between devices: 0.01 us -> 30.3 us  [exchange(): return lax.all_to_all(value, axes, 0, 0, tiled=True)]
    ppermute x6 -> x0, starting transfers between devices: 29.1 us -> none  [gather_by_shifts(): lax.ppermute(value, axis, [(i, (i + k) % count) for i in range(count)])]
    all_gather x0 -> x2, blocking collectives: none -> 23 us  [the longest x1 11.7 us: local(): grad_rows = lax.all_gather(grad, 'x', axis=0, tiled=True)]
    ppermute x6 -> x0, waiting for transfers between devices: 13.4 us -> none  [gather_by_shifts(): lax.ppermute(value, axis, [(i, (i + k) % count) for i in range(count)])]
    all_to_all x2, blocking collectives: 38.7 us -> 51.4 us  [exchange(): return lax.all_to_all(value, axes, 0, 0, tiled=True)]
    ppermute x1, starting transfers between devices: 8.6 us -> 4.19 us  [local(): other = lax.ppermute(own, 'core', [(0, 1), (1, 0)])]
    pallas_call x0 -> x1, Pallas kernels: none -> 3.76 us  [place(): pl.pallas_call(functools.partial(place_kernel, spread, ring, rows), out_s...]
  transfers between devices with their start and end apart: 9 -> 3, of which waited for: 4 -> 2; matrix products, arithmetic and copies ran while one was open for 5% -> 3% of each run, Pallas kernels for 0% -> 0%
where the time goes in v2:
time: 140 us
  blocking collectives  74.4 us (53%)
  waiting for transfers between devices  30.3 us (22%)
  starting transfers between devices  18.9 us (13%)
  other arithmetic  4.96 us (4%)
  Pallas kernels  3.76 us (3%)
  local copies, waits for them, and re-layouts  3.24 us (2%)
  matrix products  2.42 us (2%)
  between operations  2.11 us (2%)
    all_to_all x2, blocking collectives, exchange(): return lax.all_to_all(value, axes, 0, 0, tiled=True)  51.4 us
    all_to_all x2, waiting for transfers between devices, exchange(): return lax.all_to_all(value, axes, 0, 0, tiled=True)  30.3 us
    all_to_all x2, starting transfers between devices, exchange(): return lax.all_to_all(value, axes, 0, 0, tiled=True)  14.7 us
    all_gather x1, blocking collectives, local(): grad_rows = lax.all_gather(grad, 'x', axis=0, tiled=True)  11.7 us
    all_gather x1, blocking collectives, local(): left_rows = lax.all_gather(left_own, 'x', axis=0, tiled=True)  11.4 us
    ppermute x1, starting transfers between devices, local(): other = lax.ppermute(own, 'core', [(0, 1), (1, 0)])  4.19 us
    pallas_call x1, Pallas kernels, place(): pl.pallas_call(functools.partial(place_kernel, spread, ring, rows), out_s...  3.76 us
    broadcast_in_dim x3, local copies, waits for them, and re-layouts, copies(): return jnp.broadcast_to(value[None], (count,) + value.shape)  3.06 us
  transfers between devices with their start and end apart: 3, of which 2 were waited for; matrix products, arithmetic and copies ran while one was open for 3% of the time, Pallas kernels for 0%

profile of v2, /device:TPU:1, one launch (start us, length us, event | category | flops | bytes accessed | tf_op | source)
XLA Modules:
  0.0 140.1 jit_solution(5882796721206027921)
XLA Ops:
  0.6 2.0 %broadcast_in_dim.47 = f32[8,32,1024]{2,1,0:T(8,128)} broadcast(f32[32,1024]{1,0:T(8,128)} %bitcast.44), dimensions={1,2} | broadcast | bytes 1179648 | tf_op jit(solution)/shard_map/broadcast_in_dim | solution.py:24
  2.6 0.0 copy-start
  2.6 0.0 copy-start.1
  2.6 11.0 %all-to-all-start = ((f32[8,32,1024]{2,1,0:T(8,128)}), f32[8,32,1024]{2,1,0:T(8,128)S(1)}, u32[]{:S(2)}, u32[]{:S(2)}) async-start(f32[8,32,1024]{2,1,0:T(8,128)} %broadcast_in_dim.47), calls=%async_computation | async-start | bytes 2097152 | tf_op jit(solution)/shard_map/all_to_all | solution.py:20
  13.6 0.0 copy-done
  13.6 0.6 fusion.4
  14.9 0.0 copy-done.1
  14.9 1.6 %fusion.2 = (f32[1,32,1024]{2,1,0:T(8,128)}, f32[32,1024]{1,0:T(8,128)S(1)}) fusion(f32[1,32,1024]{2,1,0:T(8,128)S(1)} %copy-done.1, f32[32,16384]{1,0:T(8,128)} %param.7, s32[]{:T(128)S(6)} %select_n.8), kind=kLoop, calls=%fused_computation.7 | loop fusion | flops 131072 | bytes 524292 | tf_op jit(solution)/shard_map/broadcast_in_dim | solution.py:125
  16.5 11.7 %all_gather.6 = f32[128,1024]{1,0:T(8,128)S(1)} all-gather(f32[32,1024]{1,0:T(8,128)S(1)} %get-tuple-element.8), channel_id=1, replica_groups=mesh['z'=8,'x'=4,'y'=8,'core'=2] {'x'}, dimensions={0}, use_global_device_ids=true | all-gather | bytes 655360 | tf_op jit(solution)/shard_map/all_gather | solution.py:93
  28.2 14.6 %all-to-all-done = f32[8,32,1024]{2,1,0:T(8,128)S(1)} async-done(((f32[8,32,1024]{2,1,0:T(8,128)}), f32[8,32,1024]{2,1,0:T(8,128)S(1)}, u32[]{:S(2)}, u32[]{:S(2)}) %all-to-all-start) | async-done | bytes 1048608 | tf_op jit(solution)/shard_map/all_to_all | solution.py:20
  42.8 1.2 fusion.5
  44.0 1.1 broadcast_in_dim.48
  45.1 0.0 copy-start.2
  45.1 0.0 copy-start.3
  45.1 3.7 %all-to-all-start.1 = ((f32[8,128,256]{2,1,0:T(8,128)}), f32[8,128,256]{2,1,0:T(8,128)S(1)}, u32[]{:S(2)}, u32[]{:S(2)}) async-start(f32[8,128,256]{2,1,0:T(8,128)} %broadcast_in_dim.48), calls=%async_computation.1 | async-start | bytes 2097152 | tf_op jit(solution)/shard_map/all_to_all | solution.py:20
  49.5 0.0 copy-done.2
  49.5 1.4 fusion.1
  50.9 0.0 copy-done.3
  50.9 11.4 %all_gather.7 = f32[128,1024]{1,0:T(8,128)S(1)} all-gather(f32[32,1024]{1,0:T(8,128)S(1)} %bitcast.45), channel_id=1, replica_groups=mesh['z'=8,'x'=4,'y'=8,'core'=2] {'x'}, dimensions={0}, use_global_device_ids=true | all-gather | bytes 655360 | tf_op jit(solution)/shard_map/all_gather | solution.py:107
  62.3 15.7 %all-to-all-done.1 = f32[8,128,256]{2,1,0:T(8,128)S(1)} async-done(((f32[8,128,256]{2,1,0:T(8,128)}), f32[8,128,256]{2,1,0:T(8,128)S(1)}, u32[]{:S(2)}, u32[]{:S(2)}) %all-to-all-start.1) | async-done | bytes 1048608 | tf_op jit(solution)/shard_map/all_to_all | solution.py:20
  77.9 1.2 multiply_reduce_fusion
  79.2 0.1 reshape.49
  79.3 1.3 fusion.3
  80.6 0.1 broadcast_in_dim.50
  80.7 41.1 %all_to_all.20 = f32[32,72,128]{2,1,0:T(8,128)S(1)} all-to-all(f32[32,72,128]{2,1,0:T(8,128)S(1)} %bitcast.40), channel_id=1, replica_groups=mesh['z'=8,'x'=4,'y'=8,'core'=2] {'x','y'}, dimensions={0} | all-to-all | bytes 2359296 | tf_op jit(solution)/shard_map/all_to_all | solution.py:20
  121.8 4.2 %collective-permute-start = (f32[32,72,128]{2,1,0:T(8,128)S(1)}, f32[32,72,128]{2,1,0:T(8,128)S(1)}, u32[]{:S(2)}, u32[]{:S(2)}) collective-permute-start(f32[32,72,128]{2,1,0:T(8,128)S(1)} %all_to_all.20), channel_id=1, source_target_pairs={{0,1},{1,0},{2,3},{3,2},{4,5},{5,4},{6,7},{7,6},{8,9},{9,8},{10,11... | collective-permute-start | bytes 3538952 | tf_op jit(solution)/shard_map/ppermute | solution.py:117
  126.0 10.2 %all_to_all.21 = f32[16,8,128]{2,1,0:T(8,128)S(1)} all-to-all(f32[16,8,128]{2,1,0:T(8,128)S(1)} %broadcast_in_dim.51), channel_id=1, replica_groups=mesh['z'=8,'x'=4,'y'=8,'core'=2] {'z','core'}, dimensions={0} | all-to-all | bytes 131072 | tf_op jit(solution)/shard_map/all_to_all | solution.py:20
  136.3 0.0 collective-permute-done
  136.3 3.8 %place.1 = f32[32,16384]{1,0:T(8,128)} custom-call(s32[16]{0:T(128)S(1)} %copy-done, s32[1]{0:T(128)} %bitcast.core, f32[8,2,8,128]{3,2,1,0:T(8,128)S(1)} %bitcast.39, f32[4,8,72,128]{3,2,1,0:T(8,128)S(1)} %bitcast.37, f32[4,8,72,128]{3,2,1,0:T(8,128)S(1)} %bitcast.38), custom_call_target="tpu_custom_call" | custom-call | tf_op jit(solution)/shard_map/place/pallas_call | solution.py:61
  (5 shorter events, 0.1 us)
Async XLA Ops:
  2.6 11.0 %copy-start = (s32[16]{0:T(128)S(1)}, s32[16]{0:T(128)}, u32[]{:S(2)}) copy-start(s32[16]{0:T(128)} %table.1) | copy-start | bytes 196
  2.6 12.3 %copy-start.1 = (f32[1,32,1024]{2,1,0:T(8,128)S(1)}, f32[1,32,1024]{2,1,0:T(8,128)}, u32[]{:S(2)}) copy-start(f32[1,32,1024]{2,1,0:T(8,128)} %param.11) | copy-start | bytes 393220
  2.6 40.2 %all-to-all-start = ((f32[8,32,1024]{2,1,0:T(8,128)}), f32[8,32,1024]{2,1,0:T(8,128)S(1)}, u32[]{:S(2)}, u32[]{:S(2)}) async-start(f32[8,32,1024]{2,1,0:T(8,128)} %broadcast_in_dim.47), calls=%async_computation | async-start | bytes 2097152 | tf_op jit(solution)/shard_map/all_to_all | solution.py:20
  45.1 4.4 %copy-start.2 = (f32[1,32,1024]{2,1,0:T(8,128)S(1)}, f32[1,32,1024]{2,1,0:T(8,128)}, u32[]{:S(2)}) copy-start(f32[1,32,1024]{2,1,0:T(8,128)} %param.10) | copy-start | bytes 393220
  45.1 5.8 %copy-start.3 = (f32[1,32,1024]{2,1,0:T(8,128)S(1)}, f32[1,32,1024]{2,1,0:T(8,128)}, u32[]{:S(2)}) copy-start(f32[1,32,1024]{2,1,0:T(8,128)} %param.8) | copy-start | bytes 393220
  45.1 32.9 %all-to-all-start.1 = ((f32[8,128,256]{2,1,0:T(8,128)}), f32[8,128,256]{2,1,0:T(8,128)S(1)}, u32[]{:S(2)}, u32[]{:S(2)}) async-start(f32[8,128,256]{2,1,0:T(8,128)} %broadcast_in_dim.48), calls=%async_computation.1 | async-start | bytes 2097152 | tf_op jit(solution)/shard_map/all_to_all | solution.py:20
  121.8 14.5 %collective-permute-start = (f32[32,72,128]{2,1,0:T(8,128)S(1)}, f32[32,72,128]{2,1,0:T(8,128)S(1)}, u32[]{:S(2)}, u32[]{:S(2)}) collective-permute-start(f32[32,72,128]{2,1,0:T(8,128)S(1)} %all_to_all.20), channel_id=1, source_target_pairs={{0,1},{1,0},{2,3},{3,2},{4,5},{5,4},{6,7},{7,6},{8,9},{9,8},{10,11... | collective-permute-start | bytes 3538952 | tf_op jit(solution)/shard_map/ppermute | solution.py:117

commit v3 on v1

v3 whole, which is shorter than its diff:
```python
import functools

import jax
import jax.numpy as jnp
from jax import lax
from jax.experimental import pallas as pl
from jax.experimental.pallas import tpu as pltpu
from jax.sharding import Mesh
from jax.sharding import PartitionSpec as P

beta_one = 0.9
beta_two = 0.95
adam_eps = 1e-08
norm_eps = 1e-06
HIGHEST = lax.Precision.HIGHEST


def exchange(value, axes):
    return lax.all_to_all(value, axes, 0, 0, tiled=True)


def shifted(value, axis, by):
    count = lax.axis_size(axis)
    return lax.ppermute(value, axis, [(i, (i + by) % count) for i in range(count)])


def block_of(table, position, blocks):
    found = jnp.int32(0)
    for k in range(blocks):
        found += jnp.where(table[k] == position, k, 0)
    return found


def pick_kernel(blocks, table, position, gradient, out, arrived):
    width = out.shape[1]
    start = pl.multiple_of(block_of(table, position[0], blocks) * width, width)
    copy = pltpu.make_async_copy(gradient.at[:, pl.ds(start, width)], out, arrived)
    copy.start()
    copy.wait()


def pick(table, position, gradient, width):
    return pl.pallas_call(
        functools.partial(pick_kernel, table.shape[0]),
        out_shape=jax.ShapeDtypeStruct((gradient.shape[0], width), jnp.float32),
        in_specs=[
            pl.BlockSpec(memory_space=pltpu.SMEM),
            pl.BlockSpec(memory_space=pltpu.SMEM),
            pl.BlockSpec(memory_space=pl.ANY),
        ],
        out_specs=pl.BlockSpec(memory_space=pltpu.VMEM),
        scratch_shapes=[pltpu.SemaphoreType.DMA],
        name="pick",
    )(table, position, gradient)


def left_kernel(near, rows, left, right, adam, out):
    spread = near // 2
    tile = jnp.dot(
        left[...].reshape(near * rows, left.shape[-1]),
        right[...],
        precision=HIGHEST,
        preferred_element_type=jnp.float32,
    )
    lane = lax.broadcasted_iota(jnp.int32, (8, 128), 1)
    tail = jnp.where(lane == 0, adam[0, 0], jnp.where(lane == 1, jnp.sum(tile * tile), 0.0))
    for x in range(spread):
        for r in range(2):
            at = (x * 2 + r) * rows
            out[r * spread + x, :rows, :] = tile[at : at + rows, :]
            out[r * spread + x, rows:, :] = tail


def left_multiply(left, right, adam, near, rows):
    return pl.pallas_call(
        functools.partial(left_kernel, near, rows),
        out_shape=jax.ShapeDtypeStruct((near, rows + 8, 128), jnp.float32),
        in_specs=[
            pl.BlockSpec(memory_space=pltpu.VMEM),
            pl.BlockSpec(memory_space=pltpu.VMEM),
            pl.BlockSpec(memory_space=pltpu.SMEM),
        ],
        out_specs=pl.BlockSpec(memory_space=pltpu.VMEM),
        compiler_params=pltpu.CompilerParams(vmem_limit_bytes=32 * 1024 * 1024),
        name="left_multiply",
    )(left, right, adam)


def scale_kernel(near, rows, held, sums, out):
    total = jnp.sum(sums[...], axis=0, keepdims=True)
    factor = jnp.sqrt(total[:, 0:1]) / (jnp.sqrt(total[:, 1:2]) + norm_eps)
    for k in range(near):
        piece = held[k, :rows, :] * factor
        for y in range(out.shape[0]):
            out[y, k * rows : (k + 1) * rows, :] = piece


def scale_copies(held, sums, near, rows, ring):
    return pl.pallas_call(
        functools.partial(scale_kernel, near, rows),
        out_shape=jax.ShapeDtypeStruct((ring, near * rows, 128), jnp.float32),
        in_specs=[pl.BlockSpec(memory_space=pltpu.VMEM)] * 2,
        out_specs=pl.BlockSpec(memory_space=pltpu.VMEM),
        compiler_params=pltpu.CompilerParams(vmem_limit_bytes=32 * 1024 * 1024),
        name="scale_copies",
    )(held, sums)


def place_kernel(quarters, spread, rows, blocks, table, part, held, *rest):
    out, tiles, sent = rest[-3:]
    lane = lax.broadcasted_iota(jnp.int32, (rows, 128), 1) // rows
    copies_out = []
    for y in range(held.shape[0]):
        for r in range(2):
            pieces = []
            for x in range(spread):
                at = (r * spread + x) * rows
                pieces.append(held[y, at : at + rows, :])
            for q in range(quarters):
                tile = pieces[q]
                for x in range(spread):
                    if x != q:
                        turned = pltpu.roll(pieces[x], (x - q) % 4 * rows, 1)
                        tile = jnp.where(lane == x, turned, tile)
                at = q * 256 + r * 128
                tiles[y, :, at : at + 128] = tile
        width = tiles.shape[2]
        start = pl.multiple_of(block_of(table, 2 * y + part[0], blocks) * width, width)
        copy = pltpu.make_async_copy(tiles.at[y], out.at[:, pl.ds(start, width)], sent.at[y])
        copy.start()
        copies_out.append(copy)
    for copy in copies_out:
        copy.wait()


def place(table, part, held, update, quarters, spread, rows, width):
    blocks, ring = table.shape[0], held.shape[0]
    operands = [table, part, held] + ([] if update is None else [update])
    return pl.pallas_call(
        functools.partial(place_kernel, quarters, spread, rows, blocks),
        out_shape=jax.ShapeDtypeStruct((rows, blocks * width), jnp.float32),
        in_specs=[
            pl.BlockSpec(memory_space=pltpu.SMEM),
            pl.BlockSpec(memory_space=pltpu.SMEM),
            pl.BlockSpec(memory_space=pltpu.VMEM),
        ]
        + ([] if update is None else [pl.BlockSpec(memory_space=pl.ANY)]),
        out_specs=pl.BlockSpec(memory_space=pl.ANY),
        scratch_shapes=[
            pltpu.VMEM((ring, rows, width), jnp.float32),
            pltpu.SemaphoreType.DMA((ring,)),
        ],
        input_output_aliases={} if update is None else {3: 0},
        compiler_params=pltpu.CompilerParams(vmem_limit_bytes=32 * 1024 * 1024),
        cost_estimate=pl.CostEstimate(flops=0, bytes_accessed=2 * ring * rows * width * 4, transcendentals=0),
        name="place_own" if update is None else "place_other",
    )(*operands)


def local(gradient, left_root, right_root, first_moment, second_moment, step_count, owner_table):
    rows, width = left_root.shape[1], left_root.shape[2]
    quarters, spread, ring = lax.axis_size("q"), lax.axis_size("x"), lax.axis_size("y")
    near = 2 * spread
    core = lax.axis_index("core").astype(jnp.int32)
    position = lax.axis_index("y").astype(jnp.int32) * 2 + core
    is_own = (jnp.arange(2, dtype=jnp.int32) == lax.axis_index("r"))[None, :, None, None]

    def spread_pair(value, got):
        shape = (spread, 2) + value.shape
        return jnp.where(
            jnp.broadcast_to(is_own, shape),
            jnp.broadcast_to(value, shape),
            jnp.broadcast_to(got, shape),
        )

    grad = pick(owner_table, position[None], gradient, width)
    grad_pair = spread_pair(grad, shifted(grad, "r", 1))
    grad_rows = exchange(grad_pair, "x")
    grad_rows = jnp.transpose(grad_rows, (1, 0, 2, 3)).reshape(near * rows, width)
    right_class = lax.all_gather(right_root[0], "q", axis=0, tiled=True)

    step_value = step_count[0].astype(jnp.float32)
    first_new = beta_one * first_moment[0] + (1.0 - beta_one) * grad
    second_new = beta_two * second_moment[0] + (1.0 - beta_two) * grad * grad
    first_fix = 1.0 - jnp.power(beta_one, step_value)
    second_fix = 1.0 - jnp.power(beta_two, step_value)
    adam_step = first_new / first_fix / (jnp.sqrt(second_new / second_fix) + adam_eps)
    adam_sq = jnp.sum(adam_step * adam_step)

    left_pair = spread_pair(left_root[0], shifted(left_root[0], "r", 1))
    left_pair, grad_rows, right_class = lax.optimization_barrier(
        (left_pair, grad_rows, right_class)
    )
    left_rows = exchange(left_pair, "x")
    right_side = lax.dot_general(
        grad_rows, right_class, (((1,), (1,)), ((), ())), precision=HIGHEST
    )
    right_all = lax.all_gather(right_side, "q", axis=0, tiled=True)
    sent = left_multiply(left_rows, right_all, adam_sq.reshape(1, 1), near, rows)
    got = exchange(sent, ("r", "x"))
    near_sums = jnp.sum(got[:, rows, :], axis=0, keepdims=True)
    totals = lax.all_gather(near_sums, "q", axis=0, tiled=True)
    own = exchange(scale_copies(got, totals, near, rows, ring), "y")
    other = lax.ppermute(own, "core", [(0, 1), (1, 0)])
    update = place(owner_table, core[None], own, None, quarters, spread, rows, width)
    update = place(owner_table, 1 - core[None], other, update, quarters, spread, rows, width)
    return update, first_new[None], second_new[None]


def solution(mesh):
    fine = Mesh(mesh.devices.reshape(4, 2, 4, 8, 2), ("q", "r", "x", "y", "core"))
    near, deep = ("q", "r", "x"), ("y", "core")
    flat, owned = P(near, None), P(deep, near, None)
    return jax.shard_map(
        local,
        mesh=fine,
        in_specs=(flat, owned, owned, owned, owned, P(), P()),
        out_specs=(flat, owned, owned),
        check_vma=False,
    )
```

time: 162 us -> 125 us (0.77)
  starting transfers between devices: 49.5 us -> 29.1 us
  local copies, waits for them, and re-layouts: 10.6 us -> 0.13 us
  waiting for transfers between devices: 13.4 us -> 3.86 us
  Pallas kernels: 0 us -> 8.64 us
  other arithmetic: 8.53 us -> 3.97 us
  blocking collectives: 73.7 us -> 76.5 us
    all_gather x0 -> x3, blocking collectives: none -> 40.7 us  [the longest x1 18.7 us: local(): right_class = lax.all_gather(right_root[0], 'q', axis=0, tiled=True)]
    unnamed x2 -> x0, blocking collectives: 35 us -> none
    ppermute x6 -> x2, starting transfers between devices: 29.1 us -> 6.75 us  [shifted(): lax.ppermute(value, axis, [(i, (i + by) % count) for i in range(count)])]
    ppermute x6 -> x2, waiting for transfers between devices: 13.4 us -> 3.75 us  [shifted(): lax.ppermute(value, axis, [(i, (i + by) % count) for i in range(count)])]
    pallas_call x0 -> x5, Pallas kernels: none -> 8.64 us  [the longest x2 4.28 us: place(): pl.pallas_call(functools.partial(place_kernel, quarters, spread, rows, bl...]
    ppermute x1, starting transfers between devices: 8.6 us -> 14.6 us  [local(): other = lax.ppermute(own, 'core', [(0, 1), (1, 0)])]
    all_to_all x2, starting transfers between devices: 11.8 us -> 7.67 us  [exchange(): return lax.all_to_all(value, axes, 0, 0, tiled=True)]
    all_to_all x2, blocking collectives: 38.7 us -> 35.8 us  [exchange(): return lax.all_to_all(value, axes, 0, 0, tiled=True)]
  transfers between devices with their start and end apart: 9 -> 5, of which waited for: 4 -> 3; matrix products, arithmetic and copies ran while one was open for 5% -> 2% of each run, Pallas kernels for 0% -> 2%
where the time goes in v3:
time: 125 us
  blocking collectives  76.5 us (61%)
  starting transfers between devices  29.1 us (23%)
  Pallas kernels  8.64 us (7%)
  other arithmetic  3.97 us (3%)
  waiting for transfers between devices  3.86 us (3%)
  between operations  1.54 us (1%)
    all_to_all x2, blocking collectives, exchange(): return lax.all_to_all(value, axes, 0, 0, tiled=True)  35.8 us
    all_gather x1, blocking collectives, local(): right_class = lax.all_gather(right_root[0], 'q', axis=0, tiled=True)  18.7 us
    ppermute x1, starting transfers between devices, local(): other = lax.ppermute(own, 'core', [(0, 1), (1, 0)])  14.6 us
    all_gather x1, blocking collectives, local(): right_all = lax.all_gather(right_side, 'q', axis=0, tiled=True)  14 us
    all_gather x1, blocking collectives, local(): totals = lax.all_gather(near_sums, 'q', axis=0, tiled=True)  7.97 us
    all_to_all x2, starting transfers between devices, exchange(): return lax.all_to_all(value, axes, 0, 0, tiled=True)  7.67 us
    ppermute x2, starting transfers between devices, shifted(): lax.ppermute(value, axis, [(i, (i + by) % count) for i in range(count)])  6.75 us
    pallas_call x2, Pallas kernels, place(): pl.pallas_call(functools.partial(place_kernel, quarters, spread, rows, bl...  4.28 us
  transfers between devices with their start and end apart: 5, of which 3 were waited for; matrix products, arithmetic and copies ran while one was open for 2% of the time, Pallas kernels for 2%

profile of v3, /device:TPU:1, one launch (start us, length us, event | category | flops | bytes accessed | tf_op | source)
XLA Modules:
  0.0 124.6 jit_solution(5201950273371747236)
XLA Ops:
  0.6 0.0 copy-start.2
  0.6 2.4 %pick.1 = f32[32,1024]{1,0:T(8,128)} custom-call(s32[16]{0:T(128)} %table.5, s32[1]{0:T(128)} %bitcast.2.position, f32[32,16384]{1,0:T(8,128)} %gradient.1), custom_call_target="tpu_custom_call" | custom-call | tf_op jit(solution)/shard_map/pick/pallas_call | solution.py:43
  3.0 4.8 %collective-permute-start.1 = (f32[32,1024]{1,0:T(8,128)}, f32[32,1024]{1,0:T(8,128)S(1)}, u32[]{:S(2)}, u32[]{:S(2)}) collective-permute-start(f32[32,1024]{1,0:T(8,128)} %pick.1), channel_id=1, source_target_pairs={{0,64},{64,0},{1,65},{65,1},{2,66},{66,2},{3,67},{67,3},{4,68},{68... | collective-permute-start | bytes 393224 | tf_op jit(solution)/shard_map/ppermute | solution.py:24
  7.9 0.0 copy-done.2
  7.9 1.9 %collective-permute-start = (f32[32,1024]{1,0:T(8,128)S(1)}, f32[32,1024]{1,0:T(8,128)S(1)}, u32[]{:S(2)}, u32[]{:S(2)}) collective-permute-start(f32[32,1024]{1,0:T(8,128)S(1)} %bitcast.33), channel_id=1, source_target_pairs={{0,64},{64,0},{1,65},{65,1},{2,66},{66,2},{3,67},{67,3},{4,68},{68... | collective-permute-start | bytes 393224 | tf_op jit(solution)/shard_map/ppermute | solution.py:24
  9.8 0.0 copy-start.3
  9.8 0.6 collective-permute-done.1
  10.4 3.2 %collective-permute-done = f32[32,1024]{1,0:T(8,128)S(1)} collective-permute-done((f32[32,1024]{1,0:T(8,128)S(1)}, f32[32,1024]{1,0:T(8,128)S(1)}, u32[]{:S(2)}, u32[]{:S(2)}) %collective-permute-start) | collective-permute-done | bytes 131104 | tf_op jit(solution)/shard_map/ppermute | solution.py:24
  13.6 2.5 %broadcast_select_fusion = (f32[4,2,32,1024]{3,2,1,0:T(8,128)}, f32[4,2,32,1024]{3,2,1,0:T(8,128)}) fusion(f32[32,1024]{1,0:T(8,128)S(1)} %collective-permute-done.1, f32[32,1024]{1,0:T(8,128)} %pick.1, pred[2]{0:T(512)(128)(4,1)S(1)} %iota_compare_fusion, f32[32,1024]{1,0:T(8,128)S(1)} %collective-permute-done, f32[32,1024]{1,0:T(8,128)S(1)} %bitcast.34), kind=kLoop, calls=%fused_computation | loop fusion | flops 524288 | bytes 2621442 | tf_op jit(solution)/shard_map/jit(_where)/select_n | solution.py:170
  16.1 4.0 %all-to-all-start = ((f32[4,2,32,1024]{3,2,1,0:T(8,128)}), f32[4,2,32,1024]{3,2,1,0:T(8,128)S(1)}, u32[]{:S(2)}, u32[]{:S(2)}) async-start(f32[4,2,32,1024]{3,2,1,0:T(8,128)} %get-tuple-element.12), calls=%async_computation | async-start | bytes 2097152 | tf_op jit(solution)/shard_map/all_to_all | solution.py:19
  20.1 0.0 copy-done.3
  20.2 18.7 %all-gather = f32[1,128,1024]{2,1,0:T(8,128)S(1)} all-gather(f32[1,32,1024]{2,1,0:T(8,128)S(1)} %copy-done.3), channel_id=2, replica_groups=mesh['q'=4,'r'=2,'x'=4,'y'=8,'core'=2] {'q'}, dimensions={1}, use_global_device_ids=true | all-gather | bytes 655360 | tf_op jit(solution)/shard_map/all_gather | solution.py:180
  38.9 0.0 all-to-all-done
  38.9 0.0 copy-start.1
  38.9 0.0 copy-start.4
  38.9 0.0 copy-start.5
  38.9 0.1 copy.14
  39.0 3.7 %all-to-all-start.1 = ((f32[4,2,32,1024]{3,2,1,0:T(8,128)}), f32[4,2,32,1024]{3,2,1,0:T(8,128)S(1)}, u32[]{:S(2)}, u32[]{:S(2)}) async-start(f32[4,2,32,1024]{3,2,1,0:T(8,128)} %get-tuple-element.6), calls=%async_computation.1 | async-start | bytes 2097152 | tf_op jit(solution)/shard_map/all_to_all | solution.py:19
  43.4 0.0 copy-done.1
  43.4 0.0 copy-done.4
  43.4 0.0 copy-done.5
  43.4 1.4 %fusion.2 = (f32[1,32,1024]{2,1,0:T(8,128)}, f32[]{:T(128)}, f32[1,32,1024]{2,1,0:T(8,128)}) fusion(f32[32,1024]{1,0:T(8,128)S(1)} %copy-done.1, f32[1,32,1024]{2,1,0:T(8,128)S(1)} %copy-done.4, f32[]{:T(128)} %bitcast.9, f32[]{:T(128)} %bitcast.7, f32[1,32,1024]{2,1,0:T(8,128)S(1)} %copy-done.5), kind=kLoop, calls=%fused_computation.7 | loop fusion | flops 425983 | bytes 655372 | tf_op jit(solution)/shard_map/broadcast_in_dim | solution.py:207
  44.8 1.0 fusion.3
  45.8 14.0 %all_gather.10.right = f32[1024,128]{1,0:T(8,128)S(1)} all-gather(f32[256,128]{1,0:T(8,128)S(1)} %fusion.3), channel_id=1, replica_groups=mesh['q'=4,'r'=2,'x'=4,'y'=8,'core'=2] {'q'}, dimensions={0}, use_global_device_ids=true | all-gather | bytes 655360 | tf_op jit(solution)/shard_map/all_gather | solution.py:198
  59.8 0.0 all-to-all-done.1.left
  59.8 1.8 %left_multiply.1 = f32[8,40,128]{2,1,0:T(8,128)S(1)} custom-call(f32[4,2,32,1024]{3,2,1,0:T(8,128)S(1)} %all-to-all-done.1.left, f32[1024,128]{1,0:T(8,128)S(1)} %all_gather.10.right, f32[1,1]{1,0:T(1,128)} %bitcast.10.adam), custom_call_target="tpu_custom_call" | custom-call | tf_op jit(solution)/shard_map/left_multiply/pallas_call | solution.py:75
  61.6 0.0 copy-start
  61.6 11.3 %all_to_all.20.held = f32[8,40,128]{2,1,0:T(8,128)S(1)} all-to-all(f32[8,40,128]{2,1,0:T(8,128)S(1)} %left_multiply.1), channel_id=1, replica_groups=mesh['q'=4,'r'=2,'x'=4,'y'=8,'core'=2] {'r','x'}, dimensions={0} | all-to-all | bytes 327680 | tf_op jit(solution)/shard_map/all_to_all | solution.py:19
  72.9 8.0 %all-gather.2 = f32[4,1,128]{2,1,0:T(1,128)S(1)} all-gather(f32[1,1,128]{2,1,0:T(1,128)S(1)} %bitcast.35), channel_id=3, replica_groups=mesh['q'=4,'r'=2,'x'=4,'y'=8,'core'=2] {'q'}, dimensions={0}, use_global_device_ids=true | all-gather | bytes 2560 | tf_op jit(solution)/shard_map/all_gather | solution.py:202
  80.9 0.2 scale_copies.1
  81.1 24.5 %all_to_all.21.held = f32[8,256,128]{2,1,0:T(8,128)S(1)} all-to-all(f32[8,256,128]{2,1,0:T(8,128)S(1)} %scale_copies.1), channel_id=1, replica_groups=mesh['q'=4,'r'=2,'x'=4,'y'=8,'core'=2] {'y'}, dimensions={0} | all-to-all | bytes 2097152 | tf_op jit(solution)/shard_map/all_to_all | solution.py:19
  105.6 14.6 %collective-permute-start.2 = (f32[8,256,128]{2,1,0:T(8,128)S(1)}, f32[8,256,128]{2,1,0:T(8,128)S(1)}, u32[]{:S(2)}, u32[]{:S(2)}) collective-permute-start(f32[8,256,128]{2,1,0:T(8,128)S(1)} %all_to_all.21.held), channel_id=1, source_target_pairs={{0,1},{1,0},{2,3},{3,2},{4,5},{5,4},{6,7},{7,6},{8,9},{9,8},{10,11... | collective-permute-start | bytes 3145736 | tf_op jit(solution)/shard_map/ppermute | solution.py:204
  120.2 0.0 copy-done
  120.2 2.1 %place_own.1.rest_0_ = f32[32,16384]{1,0:T(8,128)} custom-call(s32[16]{0:T(128)S(1)} %copy-done, s32[1]{0:T(128)} %bitcast.part, f32[8,256,128]{2,1,0:T(8,128)S(1)} %all_to_all.21.held), custom_call_target="tpu_custom_call" | custom-call | bytes 2097152 | tf_op jit(solution)/shard_map/place_own/pallas_call | solution.py:139
  122.4 0.1 collective-permute-done.2.held
  122.5 2.1 %place_other.1 = f32[32,16384]{1,0:T(8,128)} custom-call(s32[16]{0:T(128)S(1)} %copy-done, s32[1]{0:T(128)S(6)} %sub.15.part, f32[8,256,128]{2,1,0:T(8,128)S(1)} %collective-permute-done.2.held, f32[32,16384]{1,0:T(8,128)} %place_own.1.rest_0_), custom_call_target="tpu_custom_call", output_to_operand_aliasing={{}: (3, {})} | custom-call | bytes 2097152 | tf_op jit(solution)/shard_map/place_other/pallas_call | solution.py:139
  (2 shorter events, 0.0 us)
Async XLA Ops:
  0.6 7.2 %copy-start.2 = (f32[1,32,1024]{2,1,0:T(8,128)S(1)}, f32[1,32,1024]{2,1,0:T(8,128)}, u32[]{:S(2)}) copy-start(f32[1,32,1024]{2,1,0:T(8,128)} %param.8) | copy-start | bytes 393220
  3.0 7.4 %collective-permute-start.1 = (f32[32,1024]{1,0:T(8,128)}, f32[32,1024]{1,0:T(8,128)S(1)}, u32[]{:S(2)}, u32[]{:S(2)}) collective-permute-start(f32[32,1024]{1,0:T(8,128)} %pick.1), channel_id=1, source_target_pairs={{0,64},{64,0},{1,65},{65,1},{2,66},{66,2},{3,67},{67,3},{4,68},{68... | collective-permute-start | bytes 393224 | tf_op jit(solution)/shard_map/ppermute | solution.py:24
  7.9 5.7 %collective-permute-start = (f32[32,1024]{1,0:T(8,128)S(1)}, f32[32,1024]{1,0:T(8,128)S(1)}, u32[]{:S(2)}, u32[]{:S(2)}) collective-permute-start(f32[32,1024]{1,0:T(8,128)S(1)} %bitcast.33), channel_id=1, source_target_pairs={{0,64},{64,0},{1,65},{65,1},{2,66},{66,2},{3,67},{67,3},{4,68},{68... | collective-permute-start | bytes 393224 | tf_op jit(solution)/shard_map/ppermute | solution.py:24
  9.8 10.3 %copy-start.3 = (f32[1,32,1024]{2,1,0:T(8,128)S(1)}, f32[1,32,1024]{2,1,0:T(8,128)}, u32[]{:S(2)}) copy-start(f32[1,32,1024]{2,1,0:T(8,128)} %param.9) | copy-start | bytes 393220
  16.1 22.7 %all-to-all-start = ((f32[4,2,32,1024]{3,2,1,0:T(8,128)}), f32[4,2,32,1024]{3,2,1,0:T(8,128)S(1)}, u32[]{:S(2)}, u32[]{:S(2)}) async-start(f32[4,2,32,1024]{3,2,1,0:T(8,128)} %get-tuple-element.12), calls=%async_computation | async-start | bytes 2097152 | tf_op jit(solution)/shard_map/all_to_all | solution.py:19
  38.9 4.5 %copy-start.1 = (f32[32,1024]{1,0:T(8,128)S(1)}, f32[32,1024]{1,0:T(8,128)}, u32[]{:S(2)}) copy-start(f32[32,1024]{1,0:T(8,128)} %pick.1) | copy-start | bytes 393220
  38.9 4.5 %copy-start.4 = (f32[1,32,1024]{2,1,0:T(8,128)S(1)}, f32[1,32,1024]{2,1,0:T(8,128)}, u32[]{:S(2)}) copy-start(f32[1,32,1024]{2,1,0:T(8,128)} %param.11) | copy-start | bytes 393220
  38.9 4.5 %copy-start.5 = (f32[1,32,1024]{2,1,0:T(8,128)S(1)}, f32[1,32,1024]{2,1,0:T(8,128)}, u32[]{:S(2)}) copy-start(f32[1,32,1024]{2,1,0:T(8,128)} %param.10) | copy-start | bytes 393220
  39.0 20.8 %all-to-all-start.1 = ((f32[4,2,32,1024]{3,2,1,0:T(8,128)}), f32[4,2,32,1024]{3,2,1,0:T(8,128)S(1)}, u32[]{:S(2)}, u32[]{:S(2)}) async-start(f32[4,2,32,1024]{3,2,1,0:T(8,128)} %get-tuple-element.6), calls=%async_computation.1 | async-start | bytes 2097152 | tf_op jit(solution)/shard_map/all_to_all | solution.py:19
  61.6 58.6 %copy-start = (s32[16]{0:T(128)S(1)}, s32[16]{0:T(128)}, u32[]{:S(2)}) copy-start(s32[16]{0:T(128)} %table.5) | copy-start | bytes 196
  105.6 16.9 %collective-permute-start.2 = (f32[8,256,128]{2,1,0:T(8,128)S(1)}, f32[8,256,128]{2,1,0:T(8,128)S(1)}, u32[]{:S(2)}, u32[]{:S(2)}) collective-permute-start(f32[8,256,128]{2,1,0:T(8,128)S(1)} %all_to_all.21.held), channel_id=1, source_target_pairs={{0,1},{1,0},{2,3},{3,2},{4,5},{5,4},{6,7},{7,6},{8,9},{9,8},{10,11... | collective-permute-start | bytes 3145736 | tf_op jit(solution)/shard_map/ppermute | solution.py:204

commit v4 on v3

--- a/solution.py
+++ b/solution.py
@@ -86,19 +86,27 @@
     )(left, right, adam)
 
 
-def scale_kernel(near, rows, held, sums, out):
+def scale_kernel(quarters, spread, rows, held, sums, out):
     total = jnp.sum(sums[...], axis=0, keepdims=True)
     factor = jnp.sqrt(total[:, 0:1]) / (jnp.sqrt(total[:, 1:2]) + norm_eps)
-    for k in range(near):
-        piece = held[k, :rows, :] * factor
-        for y in range(out.shape[0]):
-            out[y, k * rows : (k + 1) * rows, :] = piece
-
-
-def scale_copies(held, sums, near, rows, ring):
-    return pl.pallas_call(
-        functools.partial(scale_kernel, near, rows),
-        out_shape=jax.ShapeDtypeStruct((ring, near * rows, 128), jnp.float32),
+    lane = lax.broadcasted_iota(jnp.int32, (rows, 128), 1) // rows
+    for r in range(2):
+        pieces = [held[r * spread + x, :rows, :] * factor for x in range(spread)]
+        for q in range(quarters):
+            tile = pieces[q]
+            for x in range(spread):
+                if x != q:
+                    turned = pltpu.roll(pieces[x], (x - q) % 4 * rows, 1)
+                    tile = jnp.where(lane == x, turned, tile)
+            at = (q * 2 + r) * 128
+            for y in range(out.shape[0]):
+                out[y, :, at : at + 128] = tile
+
+
+def scale_copies(held, sums, quarters, spread, rows, ring, width):
+    return pl.pallas_call(
+        functools.partial(scale_kernel, quarters, spread, rows),
+        out_shape=jax.ShapeDtypeStruct((ring, rows, width), jnp.float32),
         in_specs=[pl.BlockSpec(memory_space=pltpu.VMEM)] * 2,
         out_specs=pl.BlockSpec(memory_space=pltpu.VMEM),
         compiler_params=pltpu.CompilerParams(vmem_limit_bytes=32 * 1024 * 1024),
@@ -106,38 +114,25 @@
     )(held, sums)
 
 
-def place_kernel(quarters, spread, rows, blocks, table, part, held, *rest):
-    out, tiles, sent = rest[-3:]
-    lane = lax.broadcasted_iota(jnp.int32, (rows, 128), 1) // rows
-    copies_out = []
+def place_kernel(blocks, table, part, held, *rest):
+    out, sent = rest[-2:]
+    width = held.shape[2]
+    started = []
     for y in range(held.shape[0]):
-        for r in range(2):
-            pieces = []
-            for x in range(spread):
-                at = (r * spread + x) * rows
-                pieces.append(held[y, at : at + rows, :])
-            for q in range(quarters):
-                tile = pieces[q]
-                for x in range(spread):
-                    if x != q:
-                        turned = pltpu.roll(pieces[x], (x - q) % 4 * rows, 1)
-                        tile = jnp.where(lane == x, turned, tile)
-                at = q * 256 + r * 128
-                tiles[y, :, at : at + 128] = tile
-        width = tiles.shape[2]
         start = pl.multiple_of(block_of(table, 2 * y + part[0], blocks) * width, width)
-        copy = pltpu.make_async_copy(tiles.at[y], out.at[:, pl.ds(start, width)], sent.at[y])
+        copy = pltpu.make_async_copy(held.at[y], out.at[:, pl.ds(start, width)], sent.at[y])
         copy.start()
-        copies_out.append(copy)
-    for copy in copies_out:
+        started.append(copy)
+    for copy in started:
         copy.wait()
 
 
-def place(table, part, held, update, quarters, spread, rows, width):
-    blocks, ring = table.shape[0], held.shape[0]
+def place(table, part, held, update):
+    blocks = table.shape[0]
+    ring, rows, width = held.shape
     operands = [table, part, held] + ([] if update is None else [update])
     return pl.pallas_call(
-        functools.partial(place_kernel, quarters, spread, rows, blocks),
+        functools.partial(place_kernel, blocks),
         out_shape=jax.ShapeDtypeStruct((rows, blocks * width), jnp.float32),
         in_specs=[
             pl.BlockSpec(memory_space=pltpu.SMEM),
@@ -146,13 +141,12 @@
         ]
         + ([] if update is None else [pl.BlockSpec(memory_space=pl.ANY)]),
         out_specs=pl.BlockSpec(memory_space=pl.ANY),
-        scratch_shapes=[
-            pltpu.VMEM((ring, rows, width), jnp.float32),
-            pltpu.SemaphoreType.DMA((ring,)),
-        ],
+        scratch_shapes=[pltpu.SemaphoreType.DMA((ring,))],
         input_output_aliases={} if update is None else {3: 0},
         compiler_params=pltpu.CompilerParams(vmem_limit_bytes=32 * 1024 * 1024),
-        cost_estimate=pl.CostEstimate(flops=0, bytes_accessed=2 * ring * rows * width * 4, transcendentals=0),
+        cost_estimate=pl.CostEstimate(
+            flops=0, bytes_accessed=2 * ring * rows * width * 4, transcendentals=0
+        ),
         name="place_own" if update is None else "place_other",
     )(*operands)
 
@@ -175,8 +169,6 @@
 
     grad = pick(owner_table, position[None], gradient, width)
     grad_pair = spread_pair(grad, shifted(grad, "r", 1))
-    grad_rows = exchange(grad_pair, "x")
-    grad_rows = jnp.transpose(grad_rows, (1, 0, 2, 3)).reshape(near * rows, width)
     right_class = lax.all_gather(right_root[0], "q", axis=0, tiled=True)
 
     step_value = step_count[0].astype(jnp.float32)
@@ -187,6 +179,9 @@
     adam_step = first_new / first_fix / (jnp.sqrt(second_new / second_fix) + adam_eps)
     adam_sq = jnp.sum(adam_step * adam_step)
 
+    grad_pair, adam_sq = lax.optimization_barrier((grad_pair, adam_sq))
+    grad_rows = exchange(grad_pair, "x")
+    grad_rows = jnp.transpose(grad_rows, (1, 0, 2, 3)).reshape(near * rows, width)
     left_pair = spread_pair(left_root[0], shifted(left_root[0], "r", 1))
     left_pair, grad_rows, right_class = lax.optimization_barrier(
         (left_pair, grad_rows, right_class)
@@ -200,10 +195,10 @@
     got = exchange(sent, ("r", "x"))
     near_sums = jnp.sum(got[:, rows, :], axis=0, keepdims=True)
     totals = lax.all_gather(near_sums, "q", axis=0, tiled=True)
-    own = exchange(scale_copies(got, totals, near, rows, ring), "y")
+    own = exchange(scale_copies(got, totals, quarters, spread, rows, ring, width), "y")
     other = lax.ppermute(own, "core", [(0, 1), (1, 0)])
-    update = place(owner_table, core[None], own, None, quarters, spread, rows, width)
-    update = place(owner_table, 1 - core[None], other, update, quarters, spread, rows, width)
+    update = place(owner_table, core[None], own, None)
+    update = place(owner_table, 1 - core[None], other, update)
     return update, first_new[None], second_new[None]
 
 

time: 125 us -> 122 us (0.976)
  waiting for transfers between devices: 3.86 us -> 1.33 us
    ppermute x2, waiting for transfers between devices: 3.75 us -> 0.67 us  [shifted(): lax.ppermute(value, axis, [(i, (i + by) % count) for i in range(count)])]
  transfers between devices with their start and end apart: 5 -> 5, of which waited for: 3 -> 2; matrix products, arithmetic and copies ran while one was open for 2% -> 3% of each run, Pallas kernels for 2% -> 1%
where the time goes in v4:
time: 122 us
  blocking collectives  76.4 us (63%)
  starting transfers between devices  28.9 us (24%)
  Pallas kernels  7.74 us (6%)
  other arithmetic  4.92 us (4%)
  between operations  1.52 us (1%)
  waiting for transfers between devices  1.33 us (1%)
    all_to_all x2, blocking collectives, exchange(): return lax.all_to_all(value, axes, 0, 0, tiled=True)  35.7 us
    all_gather x1, blocking collectives, local(): right_class = lax.all_gather(right_root[0], 'q', axis=0, tiled=True)  18.7 us
    ppermute x1, starting transfers between devices, local(): other = lax.ppermute(own, 'core', [(0, 1), (1, 0)])  14.6 us
    all_gather x1, blocking collectives, local(): right_all = lax.all_gather(right_side, 'q', axis=0, tiled=True)  14 us
    all_gather x1, blocking collectives, local(): totals = lax.all_gather(near_sums, 'q', axis=0, tiled=True)  7.97 us
    all_to_all x2, starting transfers between devices, exchange(): return lax.all_to_all(value, axes, 0, 0, tiled=True)  7.54 us
    ppermute x2, starting transfers between devices, shifted(): lax.ppermute(value, axis, [(i, (i + by) % count) for i in range(count)])  6.75 us
    pallas_call x2, Pallas kernels, place(): pl.pallas_call(functools.partial(place_kernel, blocks), out_shape=jax.Sha...  3.18 us
  transfers between devices with their start and end apart: 5, of which 2 were waited for; matrix products, arithmetic and copies ran while one was open for 3% of the time, Pallas kernels for 1%

profile of v4, /device:TPU:1, one launch (start us, length us, event | category | flops | bytes accessed | tf_op | source)
XLA Modules:
  0.0 122.0 jit_solution(16339819044026605266)
XLA Ops:
  0.6 0.0 copy-start.1
  0.6 0.0 copy-start.3
  0.7 0.0 copy-start.4
  0.7 2.4 %pick.1 = f32[32,1024]{1,0:T(8,128)} custom-call(s32[16]{0:T(128)} %table.5, s32[1]{0:T(128)} %bitcast.2.position, f32[32,16384]{1,0:T(8,128)} %gradient.1), custom_call_target="tpu_custom_call" | custom-call | tf_op jit(solution)/shard_map/pick/pallas_call | solution.py:43
  3.1 4.8 %collective-permute-start.1 = (f32[32,1024]{1,0:T(8,128)}, f32[32,1024]{1,0:T(8,128)S(1)}, u32[]{:S(2)}, u32[]{:S(2)}) collective-permute-start(f32[32,1024]{1,0:T(8,128)} %pick.1), channel_id=1, source_target_pairs={{0,64},{64,0},{1,65},{65,1},{2,66},{66,2},{3,67},{67,3},{4,68},{68... | collective-permute-start | bytes 393224 | tf_op jit(solution)/shard_map/ppermute | solution.py:24
  7.9 0.0 copy-done.1
  7.9 1.9 %collective-permute-start = (f32[32,1024]{1,0:T(8,128)S(1)}, f32[32,1024]{1,0:T(8,128)S(1)}, u32[]{:S(2)}, u32[]{:S(2)}) collective-permute-start(f32[32,1024]{1,0:T(8,128)S(1)} %bitcast.33), channel_id=1, source_target_pairs={{0,64},{64,0},{1,65},{65,1},{2,66},{66,2},{3,67},{67,3},{4,68},{68... | collective-permute-start | bytes 393224 | tf_op jit(solution)/shard_map/ppermute | solution.py:24
  10.6 0.0 copy-done.3
  10.6 0.0 copy-done.4
  10.6 2.4 %fusion.2 = (f32[1,32,1024]{2,1,0:T(8,128)}, f32[]{:T(128)}, f32[1,32,1024]{2,1,0:T(8,128)}) fusion(f32[32,1024]{1,0:T(8,128)} %pick.1, f32[1,32,1024]{2,1,0:T(8,128)S(1)} %copy-done.3, f32[]{:T(128)} %bitcast.6, f32[]{:T(128)} %bitcast.4, f32[1,32,1024]{2,1,0:T(8,128)S(1)} %copy-done.4), kind=kLoop, calls=%fused_computation.7 | loop fusion | flops 425983 | bytes 655372 | tf_op jit(solution)/shard_map/broadcast_in_dim | solution.py:202
  12.9 0.0 copy-start.2
  12.9 0.0 collective-permute-done.1
  13.0 0.7 collective-permute-done
  13.6 2.5 %broadcast_select_fusion = (f32[4,2,32,1024]{3,2,1,0:T(8,128)}, f32[4,2,32,1024]{3,2,1,0:T(8,128)}) fusion(f32[32,1024]{1,0:T(8,128)S(1)} %collective-permute-done.1, f32[32,1024]{1,0:T(8,128)} %pick.1, pred[2]{0:T(512)(128)(4,1)S(1)} %iota_compare_fusion, f32[32,1024]{1,0:T(8,128)S(1)} %collective-permute-done, f32[32,1024]{1,0:T(8,128)S(1)} %bitcast.34), kind=kLoop, calls=%fused_computation | loop fusion | flops 524288 | bytes 2621442 | tf_op jit(solution)/shard_map/jit(_where)/select_n | solution.py:164
  16.2 4.0 %all-to-all-start = ((f32[4,2,32,1024]{3,2,1,0:T(8,128)}), f32[4,2,32,1024]{3,2,1,0:T(8,128)S(1)}, u32[]{:S(2)}, u32[]{:S(2)}) async-start(f32[4,2,32,1024]{3,2,1,0:T(8,128)} %get-tuple-element.8), calls=%async_computation | async-start | bytes 2097152 | tf_op jit(solution)/shard_map/all_to_all | solution.py:19
  20.2 0.0 copy-done.2
  20.2 18.7 %all-gather = f32[1,128,1024]{2,1,0:T(8,128)S(1)} all-gather(f32[1,32,1024]{2,1,0:T(8,128)S(1)} %copy-done.2), channel_id=2, replica_groups=mesh['q'=4,'r'=2,'x'=4,'y'=8,'core'=2] {'q'}, dimensions={1}, use_global_device_ids=true | all-gather | bytes 655360 | tf_op jit(solution)/shard_map/all_gather | solution.py:172
  38.9 0.0 all-to-all-done
  38.9 0.1 copy.14
  39.0 3.5 %all-to-all-start.1 = ((f32[4,2,32,1024]{3,2,1,0:T(8,128)}), f32[4,2,32,1024]{3,2,1,0:T(8,128)S(1)}, u32[]{:S(2)}, u32[]{:S(2)}) async-start(f32[4,2,32,1024]{3,2,1,0:T(8,128)} %get-tuple-element.9), calls=%async_computation.1 | async-start | bytes 2097152 | tf_op jit(solution)/shard_map/all_to_all | solution.py:19
  42.6 1.0 fusion.3
  43.5 14.0 %all_gather.10.right = f32[1024,128]{1,0:T(8,128)S(1)} all-gather(f32[256,128]{1,0:T(8,128)S(1)} %fusion.3), channel_id=1, replica_groups=mesh['q'=4,'r'=2,'x'=4,'y'=8,'core'=2] {'q'}, dimensions={0}, use_global_device_ids=true | all-gather | bytes 655360 | tf_op jit(solution)/shard_map/all_gather | solution.py:193
  57.6 0.0 all-to-all-done.1.left
  57.6 1.8 %left_multiply.1 = f32[8,40,128]{2,1,0:T(8,128)S(1)} custom-call(f32[4,2,32,1024]{3,2,1,0:T(8,128)S(1)} %all-to-all-done.1.left, f32[1024,128]{1,0:T(8,128)S(1)} %all_gather.10.right, f32[1,1]{1,0:T(1,128)} %bitcast.10.adam), custom_call_target="tpu_custom_call" | custom-call | tf_op jit(solution)/shard_map/left_multiply/pallas_call | solution.py:75
  59.4 0.0 copy-start
  59.4 11.2 %all_to_all.20.held = f32[8,40,128]{2,1,0:T(8,128)S(1)} all-to-all(f32[8,40,128]{2,1,0:T(8,128)S(1)} %left_multiply.1), channel_id=1, replica_groups=mesh['q'=4,'r'=2,'x'=4,'y'=8,'core'=2] {'r','x'}, dimensions={0} | all-to-all | bytes 327680 | tf_op jit(solution)/shard_map/all_to_all | solution.py:19
  70.7 8.0 %all-gather.2 = f32[4,1,128]{2,1,0:T(1,128)S(1)} all-gather(f32[1,1,128]{2,1,0:T(1,128)S(1)} %bitcast.35), channel_id=3, replica_groups=mesh['q'=4,'r'=2,'x'=4,'y'=8,'core'=2] {'q'}, dimensions={0}, use_global_device_ids=true | all-gather | bytes 2560 | tf_op jit(solution)/shard_map/all_gather | solution.py:197
  78.6 0.3 scale_copies.1
  79.0 24.5 %all_to_all.21.held = f32[8,32,1024]{2,1,0:T(8,128)S(1)} all-to-all(f32[8,32,1024]{2,1,0:T(8,128)S(1)} %scale_copies.1), channel_id=1, replica_groups=mesh['q'=4,'r'=2,'x'=4,'y'=8,'core'=2] {'y'}, dimensions={0} | all-to-all | bytes 2097152 | tf_op jit(solution)/shard_map/all_to_all | solution.py:19
  103.5 14.6 %collective-permute-start.2 = (f32[8,32,1024]{2,1,0:T(8,128)S(1)}, f32[8,32,1024]{2,1,0:T(8,128)S(1)}, u32[]{:S(2)}, u32[]{:S(2)}) collective-permute-start(f32[8,32,1024]{2,1,0:T(8,128)S(1)} %all_to_all.21.held), channel_id=1, source_target_pairs={{0,1},{1,0},{2,3},{3,2},{4,5},{5,4},{6,7},{7,6},{8,9},{9,8},{10,11... | collective-permute-start | bytes 3145736 | tf_op jit(solution)/shard_map/ppermute | solution.py:199
  118.1 0.0 copy-done
  118.1 1.6 %place_own.1.rest_0_ = f32[32,16384]{1,0:T(8,128)} custom-call(s32[16]{0:T(128)S(1)} %copy-done, s32[1]{0:T(128)} %bitcast.part, f32[8,32,1024]{2,1,0:T(8,128)S(1)} %all_to_all.21.held), custom_call_target="tpu_custom_call" | custom-call | bytes 2097152 | tf_op jit(solution)/shard_map/place_own/pallas_call | solution.py:134
  119.7 0.7 collective-permute-done.2.held
  120.4 1.6 %place_other.1 = f32[32,16384]{1,0:T(8,128)} custom-call(s32[16]{0:T(128)S(1)} %copy-done, s32[1]{0:T(128)S(6)} %sub.15.part, f32[8,32,1024]{2,1,0:T(8,128)S(1)} %collective-permute-done.2.held, f32[32,16384]{1,0:T(8,128)} %place_own.1.rest_0_), custom_call_target="tpu_custom_call", output_to_operand_aliasing={{}: (3, {})} | custom-call | bytes 2097152 | tf_op jit(solution)/shard_map/place_other/pallas_call | solution.py:134
  (2 shorter events, 0.0 us)
Async XLA Ops:
  0.6 7.3 %copy-start.1 = (f32[1,32,1024]{2,1,0:T(8,128)S(1)}, f32[1,32,1024]{2,1,0:T(8,128)}, u32[]{:S(2)}) copy-start(f32[1,32,1024]{2,1,0:T(8,128)} %param.8) | copy-start | bytes 393220
  0.6 9.9 %copy-start.3 = (f32[1,32,1024]{2,1,0:T(8,128)S(1)}, f32[1,32,1024]{2,1,0:T(8,128)}, u32[]{:S(2)}) copy-start(f32[1,32,1024]{2,1,0:T(8,128)} %param.11) | copy-start | bytes 393220
  0.7 9.9 %copy-start.4 = (f32[1,32,1024]{2,1,0:T(8,128)S(1)}, f32[1,32,1024]{2,1,0:T(8,128)}, u32[]{:S(2)}) copy-start(f32[1,32,1024]{2,1,0:T(8,128)} %param.10) | copy-start | bytes 393220
  3.1 9.9 %collective-permute-start.1 = (f32[32,1024]{1,0:T(8,128)}, f32[32,1024]{1,0:T(8,128)S(1)}, u32[]{:S(2)}, u32[]{:S(2)}) collective-permute-start(f32[32,1024]{1,0:T(8,128)} %pick.1), channel_id=1, source_target_pairs={{0,64},{64,0},{1,65},{65,1},{2,66},{66,2},{3,67},{67,3},{4,68},{68... | collective-permute-start | bytes 393224 | tf_op jit(solution)/shard_map/ppermute | solution.py:24
  7.9 5.7 %collective-permute-start = (f32[32,1024]{1,0:T(8,128)S(1)}, f32[32,1024]{1,0:T(8,128)S(1)}, u32[]{:S(2)}, u32[]{:S(2)}) collective-permute-start(f32[32,1024]{1,0:T(8,128)S(1)} %bitcast.33), channel_id=1, source_target_pairs={{0,64},{64,0},{1,65},{65,1},{2,66},{66,2},{3,67},{67,3},{4,68},{68... | collective-permute-start | bytes 393224 | tf_op jit(solution)/shard_map/ppermute | solution.py:24
  12.9 7.2 %copy-start.2 = (f32[1,32,1024]{2,1,0:T(8,128)S(1)}, f32[1,32,1024]{2,1,0:T(8,128)}, u32[]{:S(2)}) copy-start(f32[1,32,1024]{2,1,0:T(8,128)} %param.9) | copy-start | bytes 393220
  16.2 22.7 %all-to-all-start = ((f32[4,2,32,1024]{3,2,1,0:T(8,128)}), f32[4,2,32,1024]{3,2,1,0:T(8,128)S(1)}, u32[]{:S(2)}, u32[]{:S(2)}) async-start(f32[4,2,32,1024]{3,2,1,0:T(8,128)} %get-tuple-element.8), calls=%async_computation | async-start | bytes 2097152 | tf_op jit(solution)/shard_map/all_to_all | solution.py:19
  39.0 18.5 %all-to-all-start.1 = ((f32[4,2,32,1024]{3,2,1,0:T(8,128)}), f32[4,2,32,1024]{3,2,1,0:T(8,128)S(1)}, u32[]{:S(2)}, u32[]{:S(2)}) async-start(f32[4,2,32,1024]{3,2,1,0:T(8,128)} %get-tuple-element.9), calls=%async_computation.1 | async-start | bytes 2097152 | tf_op jit(solution)/shard_map/all_to_all | solution.py:19
  59.4 58.7 %copy-start = (s32[16]{0:T(128)S(1)}, s32[16]{0:T(128)}, u32[]{:S(2)}) copy-start(s32[16]{0:T(128)} %table.5) | copy-start | bytes 196
  103.5 16.9 %collective-permute-start.2 = (f32[8,32,1024]{2,1,0:T(8,128)S(1)}, f32[8,32,1024]{2,1,0:T(8,128)S(1)}, u32[]{:S(2)}, u32[]{:S(2)}) collective-permute-start(f32[8,32,1024]{2,1,0:T(8,128)S(1)} %all_to_all.21.held), channel_id=1, source_target_pairs={{0,1},{1,0},{2,3},{3,2},{4,5},{5,4},{6,7},{7,6},{8,9},{9,8},{10,11... | collective-permute-start | bytes 3145736 | tf_op jit(solution)/shard_map/ppermute | solution.py:199

commit v5 on v4

--- a/solution.py
+++ b/solution.py
@@ -86,12 +86,10 @@
     )(left, right, adam)
 
 
-def scale_kernel(quarters, spread, rows, held, sums, out):
-    total = jnp.sum(sums[...], axis=0, keepdims=True)
-    factor = jnp.sqrt(total[:, 0:1]) / (jnp.sqrt(total[:, 1:2]) + norm_eps)
+def order_kernel(quarters, spread, rows, held, out):
     lane = lax.broadcasted_iota(jnp.int32, (rows, 128), 1) // rows
     for r in range(2):
-        pieces = [held[r * spread + x, :rows, :] * factor for x in range(spread)]
+        pieces = [held[r * spread + x, :rows, :] for x in range(spread)]
         for q in range(quarters):
             tile = pieces[q]
             for x in range(spread):
@@ -103,34 +101,37 @@
                 out[y, :, at : at + 128] = tile
 
 
-def scale_copies(held, sums, quarters, spread, rows, ring, width):
-    return pl.pallas_call(
-        functools.partial(scale_kernel, quarters, spread, rows),
+def order_copies(held, quarters, spread, rows, ring, width):
+    return pl.pallas_call(
+        functools.partial(order_kernel, quarters, spread, rows),
         out_shape=jax.ShapeDtypeStruct((ring, rows, width), jnp.float32),
-        in_specs=[pl.BlockSpec(memory_space=pltpu.VMEM)] * 2,
+        in_specs=[pl.BlockSpec(memory_space=pltpu.VMEM)],
         out_specs=pl.BlockSpec(memory_space=pltpu.VMEM),
         compiler_params=pltpu.CompilerParams(vmem_limit_bytes=32 * 1024 * 1024),
-        name="scale_copies",
-    )(held, sums)
-
-
-def place_kernel(blocks, table, part, held, *rest):
-    out, sent = rest[-2:]
+        name="order_copies",
+    )(held)
+
+
+def place_kernel(blocks, table, part, sums, held, *rest):
+    out, tiles, sent = rest[-3:]
     width = held.shape[2]
     started = []
     for y in range(held.shape[0]):
+        total = sums[pl.ds(2 * y + part[0], 1), :]
+        factor = jnp.sqrt(total[:, 0:1]) / (jnp.sqrt(total[:, 1:2]) + norm_eps)
+        tiles[y] = held[y] * factor
         start = pl.multiple_of(block_of(table, 2 * y + part[0], blocks) * width, width)
-        copy = pltpu.make_async_copy(held.at[y], out.at[:, pl.ds(start, width)], sent.at[y])
+        copy = pltpu.make_async_copy(tiles.at[y], out.at[:, pl.ds(start, width)], sent.at[y])
         copy.start()
         started.append(copy)
     for copy in started:
         copy.wait()
 
 
-def place(table, part, held, update):
+def place(table, part, sums, held, update):
     blocks = table.shape[0]
     ring, rows, width = held.shape
-    operands = [table, part, held] + ([] if update is None else [update])
+    operands = [table, part, sums, held] + ([] if update is None else [update])
     return pl.pallas_call(
         functools.partial(place_kernel, blocks),
         out_shape=jax.ShapeDtypeStruct((rows, blocks * width), jnp.float32),
@@ -138,11 +139,15 @@
             pl.BlockSpec(memory_space=pltpu.SMEM),
             pl.BlockSpec(memory_space=pltpu.SMEM),
             pl.BlockSpec(memory_space=pltpu.VMEM),
+            pl.BlockSpec(memory_space=pltpu.VMEM),
         ]
         + ([] if update is None else [pl.BlockSpec(memory_space=pl.ANY)]),
         out_specs=pl.BlockSpec(memory_space=pl.ANY),
-        scratch_shapes=[pltpu.SemaphoreType.DMA((ring,))],
-        input_output_aliases={} if update is None else {3: 0},
+        scratch_shapes=[
+            pltpu.VMEM((ring, rows, width), jnp.float32),
+            pltpu.SemaphoreType.DMA((ring,)),
+        ],
+        input_output_aliases={} if update is None else {4: 0},
         compiler_params=pltpu.CompilerParams(vmem_limit_bytes=32 * 1024 * 1024),
         cost_estimate=pl.CostEstimate(
             flops=0, bytes_accessed=2 * ring * rows * width * 4, transcendentals=0
@@ -179,10 +184,11 @@
     adam_step = first_new / first_fix / (jnp.sqrt(second_new / second_fix) + adam_eps)
     adam_sq = jnp.sum(adam_step * adam_step)
 
-    grad_pair, adam_sq = lax.optimization_barrier((grad_pair, adam_sq))
+    left_got = shifted(left_root[0], "r", 1)
+    grad_pair, left_got, adam_sq = lax.optimization_barrier((grad_pair, left_got, adam_sq))
     grad_rows = exchange(grad_pair, "x")
     grad_rows = jnp.transpose(grad_rows, (1, 0, 2, 3)).reshape(near * rows, width)
-    left_pair = spread_pair(left_root[0], shifted(left_root[0], "r", 1))
+    left_pair = spread_pair(left_root[0], left_got)
     left_pair, grad_rows, right_class = lax.optimization_barrier(
         (left_pair, grad_rows, right_class)
     )
@@ -195,10 +201,13 @@
     got = exchange(sent, ("r", "x"))
     near_sums = jnp.sum(got[:, rows, :], axis=0, keepdims=True)
     totals = lax.all_gather(near_sums, "q", axis=0, tiled=True)
-    own = exchange(scale_copies(got, totals, quarters, spread, rows, ring, width), "y")
+    own = exchange(order_copies(got, quarters, spread, rows, ring, width), "y")
+    totals = jnp.sum(totals, axis=0, keepdims=True)
+    all_sums = lax.all_gather(totals, ("y", "core"), axis=0, tiled=True)
+    own, all_sums = lax.optimization_barrier((own, all_sums))
     other = lax.ppermute(own, "core", [(0, 1), (1, 0)])
-    update = place(owner_table, core[None], own, None)
-    update = place(owner_table, 1 - core[None], other, update)
+    update = place(owner_table, core[None], all_sums, own, None)
+    update = place(owner_table, 1 - core[None], all_sums, other, update)
     return update, first_new[None], second_new[None]
 
 

time: 122 us -> 122 us (level)
  starting transfers between devices: 28.9 us -> 24.1 us
  blocking collectives: 76.4 us -> 79.9 us
    all_gather x0 -> x1, blocking collectives: none -> 28.8 us  [local(): all_sums = lax.all_gather(totals, ('y', 'core'), axis=0, tiled=True)]
    all_to_all x2 -> x1, blocking collectives: 35.7 us -> 11.3 us  [exchange(): return lax.all_to_all(value, axes, 0, 0, tiled=True)]
    ppermute x1, starting transfers between devices: 14.6 us -> 2.11 us  [local(): other = lax.ppermute(own, 'core', [(0, 1), (1, 0)])]
    all_to_all x2 -> x3, starting transfers between devices: 7.54 us -> 15.1 us  [exchange(): return lax.all_to_all(value, axes, 0, 0, tiled=True)]
    all_gather x1, blocking collectives: 14 us -> 12.5 us  [local(): right_all = lax.all_gather(right_side, 'q', axis=0, tiled=True)]
    select_n x1 -> x2, other arithmetic: 2.54 us -> 3.2 us  [spread_pair(): jnp.where(jnp.broadcast_to(is_own, shape), jnp.broadcast_to(value, shape)...]
  transfers between devices with their start and end apart: 5 -> 6, of which waited for: 2 -> 1; matrix products, arithmetic and copies ran while one was open for 3% -> 5% of each run, Pallas kernels for 1% -> 1%
where the time goes in v5:
time: 122 us
  blocking collectives  79.9 us (65%)
  starting transfers between devices  24.1 us (20%)
  Pallas kernels  8.73 us (7%)
  other arithmetic  5.6 us (5%)
  between operations  1.51 us (1%)
    all_gather x1, blocking collectives, local(): all_sums = lax.all_gather(totals, ('y', 'core'), axis=0, tiled=True)  28.8 us
    all_gather x1, blocking collectives, local(): right_class = lax.all_gather(right_root[0], 'q', axis=0, tiled=True)  18.9 us
    all_to_all x3, starting transfers between devices, exchange(): return lax.all_to_all(value, axes, 0, 0, tiled=True)  15.1 us
    all_gather x1, blocking collectives, local(): right_all = lax.all_gather(right_side, 'q', axis=0, tiled=True)  12.5 us
    all_to_all x1, blocking collectives, exchange(): return lax.all_to_all(value, axes, 0, 0, tiled=True)  11.3 us
    all_gather x1, blocking collectives, local(): totals = lax.all_gather(near_sums, 'q', axis=0, tiled=True)  8.41 us
    ppermute x2, starting transfers between devices, shifted(): lax.ppermute(value, axis, [(i, (i + by) % count) for i in range(count)])  6.88 us
    pallas_call x2, Pallas kernels, place(): pl.pallas_call(functools.partial(place_kernel, blocks), out_shape=jax.Sha...  3.38 us
  transfers between devices with their start and end apart: 6, of which 1 were waited for; matrix products, arithmetic and copies ran while one was open for 5% of the time, Pallas kernels for 1%

profile of v5, /device:TPU:1, one launch (start us, length us, event | category | flops | bytes accessed | tf_op | source)
XLA Modules:
  0.0 121.6 jit_solution(13321823219429079477)
XLA Ops:
  0.6 0.0 copy-start.2
  0.6 0.0 copy-start.3
  0.7 0.0 copy-start.4
  0.7 2.4 %pick.1 = f32[32,1024]{1,0:T(8,128)} custom-call(s32[16]{0:T(128)} %table.5, s32[1]{0:T(128)} %bitcast.2.position, f32[32,16384]{1,0:T(8,128)} %gradient.1), custom_call_target="tpu_custom_call" | custom-call | tf_op jit(solution)/shard_map/pick/pallas_call | solution.py:43
  3.1 0.0 copy-start.1
  3.1 5.0 %collective-permute-start = (f32[32,1024]{1,0:T(8,128)}, f32[32,1024]{1,0:T(8,128)S(1)}, u32[]{:S(2)}, u32[]{:S(2)}) collective-permute-start(f32[32,1024]{1,0:T(8,128)} %pick.1), channel_id=1, source_target_pairs={{0,64},{64,0},{1,65},{65,1},{2,66},{66,2},{3,67},{67,3},{4,68},{68... | collective-permute-start | bytes 393224 | tf_op jit(solution)/shard_map/ppermute | solution.py:24
  8.0 0.0 copy-done.2
  8.1 1.9 %collective-permute-start.1 = (f32[32,1024]{1,0:T(8,128)S(1)}, f32[32,1024]{1,0:T(8,128)S(1)}, u32[]{:S(2)}, u32[]{:S(2)}) collective-permute-start(f32[32,1024]{1,0:T(8,128)S(1)} %bitcast.35), channel_id=1, source_target_pairs={{0,64},{64,0},{1,65},{65,1},{2,66},{66,2},{3,67},{67,3},{4,68},{68... | collective-permute-start | bytes 393224 | tf_op jit(solution)/shard_map/ppermute | solution.py:24
  10.7 0.0 copy-done.3
  10.7 0.0 copy-done.4
  10.7 2.3 %fusion.2 = (f32[1,32,1024]{2,1,0:T(8,128)}, f32[]{:T(128)}, f32[1,32,1024]{2,1,0:T(8,128)}) fusion(f32[32,1024]{1,0:T(8,128)} %pick.1, f32[1,32,1024]{2,1,0:T(8,128)S(1)} %copy-done.3, f32[]{:T(128)} %bitcast.6, f32[]{:T(128)} %bitcast.4, f32[1,32,1024]{2,1,0:T(8,128)S(1)} %copy-done.4), kind=kLoop, calls=%fused_computation.7 | loop fusion | flops 425983 | bytes 655372 | tf_op jit(solution)/shard_map/broadcast_in_dim | solution.py:211
  13.1 0.0 collective-permute-done
  13.1 2.1 %broadcast_select_fusion.1 = f32[4,2,32,1024]{3,2,1,0:T(8,128)} fusion(f32[32,1024]{1,0:T(8,128)S(1)} %collective-permute-done, f32[32,1024]{1,0:T(8,128)} %pick.1, pred[2]{0:T(512)(128)(4,1)S(1)} %iota_compare_fusion), kind=kLoop, calls=%fused_computation.1 | loop fusion | flops 262144 | bytes 1310722 | tf_op jit(solution)/shard_map/jit(_where)/select_n | solution.py:169
  15.1 0.0 collective-permute-done.1
  15.1 4.0 %all-to-all-start = ((f32[4,2,32,1024]{3,2,1,0:T(8,128)}), f32[4,2,32,1024]{3,2,1,0:T(8,128)S(1)}, u32[]{:S(2)}, u32[]{:S(2)}) async-start(f32[4,2,32,1024]{3,2,1,0:T(8,128)} %broadcast_select_fusion.1), calls=%async_computation | async-start | bytes 2097152 | tf_op jit(solution)/shard_map/all_to_all | solution.py:19
  19.2 0.0 copy-done.1
  19.2 18.9 %all-gather = f32[1,128,1024]{2,1,0:T(8,128)S(1)} all-gather(f32[1,32,1024]{2,1,0:T(8,128)S(1)} %copy-done.1), channel_id=2, replica_groups=mesh['q'=4,'r'=2,'x'=4,'y'=8,'core'=2] {'q'}, dimensions={1}, use_global_device_ids=true | all-gather | bytes 655360 | tf_op jit(solution)/shard_map/all_gather | solution.py:177
  38.1 1.1 broadcast_select_fusion
  39.2 0.0 all-to-all-done
  39.2 0.1 copy.14
  39.3 4.3 %all-to-all-start.1 = ((f32[4,2,32,1024]{3,2,1,0:T(8,128)}), f32[4,2,32,1024]{3,2,1,0:T(8,128)S(1)}, u32[]{:S(2)}, u32[]{:S(2)}) async-start(f32[4,2,32,1024]{3,2,1,0:T(8,128)} %broadcast_select_fusion), calls=%async_computation.1 | async-start | bytes 2097152 | tf_op jit(solution)/shard_map/all_to_all | solution.py:19
  43.6 1.0 fusion.3
  44.6 12.5 %all_gather.13.right = f32[1024,128]{1,0:T(8,128)S(1)} all-gather(f32[256,128]{1,0:T(8,128)S(1)} %fusion.3), channel_id=1, replica_groups=mesh['q'=4,'r'=2,'x'=4,'y'=8,'core'=2] {'q'}, dimensions={0}, use_global_device_ids=true | all-gather | bytes 655360 | tf_op jit(solution)/shard_map/all_gather | solution.py:199
  57.0 0.0 all-to-all-done.1.left
  57.0 1.8 %left_multiply.1 = f32[8,40,128]{2,1,0:T(8,128)S(1)} custom-call(f32[4,2,32,1024]{3,2,1,0:T(8,128)S(1)} %all-to-all-done.1.left, f32[1024,128]{1,0:T(8,128)S(1)} %all_gather.13.right, f32[1,1]{1,0:T(1,128)} %bitcast.10.adam), custom_call_target="tpu_custom_call" | custom-call | tf_op jit(solution)/shard_map/left_multiply/pallas_call | solution.py:75
  58.8 0.0 copy-start
  58.8 11.3 %all_to_all.20.held = f32[8,40,128]{2,1,0:T(8,128)S(1)} all-to-all(f32[8,40,128]{2,1,0:T(8,128)S(1)} %left_multiply.1), channel_id=1, replica_groups=mesh['q'=4,'r'=2,'x'=4,'y'=8,'core'=2] {'r','x'}, dimensions={0} | all-to-all | bytes 327680 | tf_op jit(solution)/shard_map/all_to_all | solution.py:19
  70.1 1.2 order_copies.1
  71.3 6.8 %all-to-all-start.3 = ((f32[8,32,1024]{2,1,0:T(8,128)}), f32[8,32,1024]{2,1,0:T(8,128)S(1)}, u32[]{:S(2)}, u32[]{:S(2)}) async-start(f32[8,32,1024]{2,1,0:T(8,128)} %order_copies.1), calls=%async_computation.3 | async-start | bytes 2097152 | tf_op jit(solution)/shard_map/all_to_all | solution.py:19
  78.1 8.4 %all-gather.3 = f32[4,1,128]{2,1,0:T(1,128)S(1)} all-gather(f32[1,1,128]{2,1,0:T(1,128)S(1)} %bitcast.37), channel_id=3, replica_groups=mesh['q'=4,'r'=2,'x'=4,'y'=8,'core'=2] {'q'}, dimensions={0}, use_global_device_ids=true | all-gather | bytes 2560 | tf_op jit(solution)/shard_map/all_gather | solution.py:203
  86.6 28.8 %all-gather.4 = f32[16,1,128]{2,1,0:T(1,128)S(1)} all-gather(f32[1,1,128]{2,1,0:T(1,128)S(1)} %bitcast.38), channel_id=4, replica_groups=mesh['q'=4,'r'=2,'x'=4,'y'=8,'core'=2] {'y','core'}, dimensions={0}, use_global_device_ids=true | all-gather | bytes 8704 | tf_op jit(solution)/shard_map/all_gather | solution.py:206
  115.4 0.0 all-to-all-done.3.held
  115.4 2.1 %collective-permute-start.2 = (f32[8,32,1024]{2,1,0:T(8,128)S(1)}, f32[8,32,1024]{2,1,0:T(8,128)S(1)}, u32[]{:S(2)}, u32[]{:S(2)}) collective-permute-start(f32[8,32,1024]{2,1,0:T(8,128)S(1)} %all-to-all-done.3.held), channel_id=1, source_target_pairs={{0,1},{1,0},{2,3},{3,2},{4,5},{5,4},{6,7},{7,6},{8,9},{9,8},{10,11... | collective-permute-start | bytes 3145736 | tf_op jit(solution)/shard_map/ppermute | solution.py:208
  117.5 0.0 copy-done
  117.5 1.7 %place_own.1.rest_0_ = f32[32,16384]{1,0:T(8,128)} custom-call(s32[16]{0:T(128)S(1)} %copy-done, s32[1]{0:T(128)} %bitcast.part, f32[16,128]{1,0:T(8,128)S(1)} %bitcast.30, f32[8,32,1024]{2,1,0:T(8,128)S(1)} %all-to-all-done.3.held), custom_call_target="tpu_custom_call" | custom-call | bytes 2097152 | tf_op jit(solution)/shard_map/place_own/pallas_call | solution.py:135
  119.2 0.7 collective-permute-done.2.held
  119.9 1.7 %place_other.1 = f32[32,16384]{1,0:T(8,128)} custom-call(s32[16]{0:T(128)S(1)} %copy-done, s32[1]{0:T(128)S(6)} %sub.15.part, f32[16,128]{1,0:T(8,128)S(1)} %bitcast.31, f32[8,32,1024]{2,1,0:T(8,128)S(1)} %collective-permute-done.2.held, f32[32,16384]{1,0:T(8,128)} %place_own.1.rest_0_), custom_call_target="tpu_custom_call", output_to_operand_aliasing={{}: (4, {})} | custom-call | bytes 2097152 | tf_op jit(solution)/shard_map/place_other/pallas_call | solution.py:135
  (3 shorter events, 0.1 us)
Async XLA Ops:
  0.6 7.4 %copy-start.2 = (f32[1,32,1024]{2,1,0:T(8,128)S(1)}, f32[1,32,1024]{2,1,0:T(8,128)}, u32[]{:S(2)}) copy-start(f32[1,32,1024]{2,1,0:T(8,128)} %param.8) | copy-start | bytes 393220
  0.6 10.1 %copy-start.3 = (f32[1,32,1024]{2,1,0:T(8,128)S(1)}, f32[1,32,1024]{2,1,0:T(8,128)}, u32[]{:S(2)}) copy-start(f32[1,32,1024]{2,1,0:T(8,128)} %param.11) | copy-start | bytes 393220
  0.7 10.1 %copy-start.4 = (f32[1,32,1024]{2,1,0:T(8,128)S(1)}, f32[1,32,1024]{2,1,0:T(8,128)}, u32[]{:S(2)}) copy-start(f32[1,32,1024]{2,1,0:T(8,128)} %param.10) | copy-start | bytes 393220
  3.1 16.1 %copy-start.1 = (f32[1,32,1024]{2,1,0:T(8,128)S(1)}, f32[1,32,1024]{2,1,0:T(8,128)}, u32[]{:S(2)}) copy-start(f32[1,32,1024]{2,1,0:T(8,128)} %param.9) | copy-start | bytes 393220
  3.1 10.0 %collective-permute-start = (f32[32,1024]{1,0:T(8,128)}, f32[32,1024]{1,0:T(8,128)S(1)}, u32[]{:S(2)}, u32[]{:S(2)}) collective-permute-start(f32[32,1024]{1,0:T(8,128)} %pick.1), channel_id=1, source_target_pairs={{0,64},{64,0},{1,65},{65,1},{2,66},{66,2},{3,67},{67,3},{4,68},{68... | collective-permute-start | bytes 393224 | tf_op jit(solution)/shard_map/ppermute | solution.py:24
  8.1 7.1 %collective-permute-start.1 = (f32[32,1024]{1,0:T(8,128)S(1)}, f32[32,1024]{1,0:T(8,128)S(1)}, u32[]{:S(2)}, u32[]{:S(2)}) collective-permute-start(f32[32,1024]{1,0:T(8,128)S(1)} %bitcast.35), channel_id=1, source_target_pairs={{0,64},{64,0},{1,65},{65,1},{2,66},{66,2},{3,67},{67,3},{4,68},{68... | collective-permute-start | bytes 393224 | tf_op jit(solution)/shard_map/ppermute | solution.py:24
  15.1 24.1 %all-to-all-start = ((f32[4,2,32,1024]{3,2,1,0:T(8,128)}), f32[4,2,32,1024]{3,2,1,0:T(8,128)S(1)}, u32[]{:S(2)}, u32[]{:S(2)}) async-start(f32[4,2,32,1024]{3,2,1,0:T(8,128)} %broadcast_select_fusion.1), calls=%async_computation | async-start | bytes 2097152 | tf_op jit(solution)/shard_map/all_to_all | solution.py:19
  39.3 17.7 %all-to-all-start.1 = ((f32[4,2,32,1024]{3,2,1,0:T(8,128)}), f32[4,2,32,1024]{3,2,1,0:T(8,128)S(1)}, u32[]{:S(2)}, u32[]{:S(2)}) async-start(f32[4,2,32,1024]{3,2,1,0:T(8,128)} %broadcast_select_fusion), calls=%async_computation.1 | async-start | bytes 2097152 | tf_op jit(solution)/shard_map/all_to_all | solution.py:19
  58.8 58.7 %copy-start = (s32[16]{0:T(128)S(1)}, s32[16]{0:T(128)}, u32[]{:S(2)}) copy-start(s32[16]{0:T(128)} %table.5) | copy-start | bytes 196
  71.3 44.1 %all-to-all-start.3 = ((f32[8,32,1024]{2,1,0:T(8,128)}), f32[8,32,1024]{2,1,0:T(8,128)S(1)}, u32[]{:S(2)}, u32[]{:S(2)}) async-start(f32[8,32,1024]{2,1,0:T(8,128)} %order_copies.1), calls=%async_computation.3 | async-start | bytes 2097152 | tf_op jit(solution)/shard_map/all_to_all | solution.py:19
  115.4 4.5 %collective-permute-start.2 = (f32[8,32,1024]{2,1,0:T(8,128)S(1)}, f32[8,32,1024]{2,1,0:T(8,128)S(1)}, u32[]{:S(2)}, u32[]{:S(2)}) collective-permute-start(f32[8,32,1024]{2,1,0:T(8,128)S(1)} %all-to-all-done.3.held), channel_id=1, source_target_pairs={{0,1},{1,0},{2,3},{3,2},{4,5},{5,4},{6,7},{7,6},{8,9},{9,8},{10,11... | collective-permute-start | bytes 3145736 | tf_op jit(solution)/shard_map/ppermute | solution.py:208

commit v6 on v5

--- a/solution.py
+++ b/solution.py
@@ -31,27 +31,27 @@
     return found
 
 
-def pick_kernel(blocks, table, position, gradient, out, arrived):
+def pick_kernel(blocks, table, gradient, out, arrived):
     width = out.shape[1]
-    start = pl.multiple_of(block_of(table, position[0], blocks) * width, width)
+    position = lax.axis_index("y") * 2 + lax.axis_index("core")
+    start = pl.multiple_of(block_of(table, position, blocks) * width, width)
     copy = pltpu.make_async_copy(gradient.at[:, pl.ds(start, width)], out, arrived)
     copy.start()
     copy.wait()
 
 
-def pick(table, position, gradient, width):
+def pick(table, gradient, width):
     return pl.pallas_call(
         functools.partial(pick_kernel, table.shape[0]),
         out_shape=jax.ShapeDtypeStruct((gradient.shape[0], width), jnp.float32),
         in_specs=[
-            pl.BlockSpec(memory_space=pltpu.SMEM),
             pl.BlockSpec(memory_space=pltpu.SMEM),
             pl.BlockSpec(memory_space=pl.ANY),
         ],
         out_specs=pl.BlockSpec(memory_space=pltpu.VMEM),
         scratch_shapes=[pltpu.SemaphoreType.DMA],
         name="pick",
-    )(table, position, gradient)
+    )(table, gradient)
 
 
 def left_kernel(near, rows, left, right, adam, out):
@@ -112,15 +112,17 @@
     )(held)
 
 
-def place_kernel(blocks, table, part, sums, held, *rest):
+def place_kernel(blocks, table, sums, held, *rest):
     out, tiles, sent = rest[-3:]
+    core = lax.axis_index("core")
+    part = core if len(rest) == 3 else 1 - core
     width = held.shape[2]
     started = []
     for y in range(held.shape[0]):
-        total = sums[pl.ds(2 * y + part[0], 1), :]
+        total = sums[pl.ds(2 * y + part, 1), :]
         factor = jnp.sqrt(total[:, 0:1]) / (jnp.sqrt(total[:, 1:2]) + norm_eps)
         tiles[y] = held[y] * factor
-        start = pl.multiple_of(block_of(table, 2 * y + part[0], blocks) * width, width)
+        start = pl.multiple_of(block_of(table, 2 * y + part, blocks) * width, width)
         copy = pltpu.make_async_copy(tiles.at[y], out.at[:, pl.ds(start, width)], sent.at[y])
         copy.start()
         started.append(copy)
@@ -128,15 +130,14 @@
         copy.wait()
 
 
-def place(table, part, sums, held, update):
+def place(table, sums, held, update):
     blocks = table.shape[0]
     ring, rows, width = held.shape
-    operands = [table, part, sums, held] + ([] if update is None else [update])
+    operands = [table, sums, held] + ([] if update is None else [update])
     return pl.pallas_call(
         functools.partial(place_kernel, blocks),
         out_shape=jax.ShapeDtypeStruct((rows, blocks * width), jnp.float32),
         in_specs=[
-            pl.BlockSpec(memory_space=pltpu.SMEM),
             pl.BlockSpec(memory_space=pltpu.SMEM),
             pl.BlockSpec(memory_space=pltpu.VMEM),
             pl.BlockSpec(memory_space=pltpu.VMEM),
@@ -147,7 +148,7 @@
             pltpu.VMEM((ring, rows, width), jnp.float32),
             pltpu.SemaphoreType.DMA((ring,)),
         ],
-        input_output_aliases={} if update is None else {4: 0},
+        input_output_aliases={} if update is None else {3: 0},
         compiler_params=pltpu.CompilerParams(vmem_limit_bytes=32 * 1024 * 1024),
         cost_estimate=pl.CostEstimate(
             flops=0, bytes_accessed=2 * ring * rows * width * 4, transcendentals=0
@@ -160,8 +161,6 @@
     rows, width = left_root.shape[1], left_root.shape[2]
     quarters, spread, ring = lax.axis_size("q"), lax.axis_size("x"), lax.axis_size("y")
     near = 2 * spread
-    core = lax.axis_index("core").astype(jnp.int32)
-    position = lax.axis_index("y").astype(jnp.int32) * 2 + core
     is_own = (jnp.arange(2, dtype=jnp.int32) == lax.axis_index("r"))[None, :, None, None]
 
     def spread_pair(value, got):
@@ -172,7 +171,7 @@
             jnp.broadcast_to(got, shape),
         )
 
-    grad = pick(owner_table, position[None], gradient, width)
+    grad = pick(owner_table, gradient, width)
     grad_pair = spread_pair(grad, shifted(grad, "r", 1))
     right_class = lax.all_gather(right_root[0], "q", axis=0, tiled=True)
 
@@ -206,8 +205,8 @@
     all_sums = lax.all_gather(totals, ("y", "core"), axis=0, tiled=True)
     own, all_sums = lax.optimization_barrier((own, all_sums))
     other = lax.ppermute(own, "core", [(0, 1), (1, 0)])
-    update = place(owner_table, core[None], all_sums, own, None)
-    update = place(owner_table, 1 - core[None], all_sums, other, update)
+    update = place(owner_table, all_sums, own, None)
+    update = place(owner_table, all_sums, other, update)
     return update, first_new[None], second_new[None]
 
 

time: 122 us -> 122 us (level)
  no operation moved by 1% of the time
where the time goes in v6:
time: 122 us
  blocking collectives  79.9 us (65%)
  starting transfers between devices  24.1 us (20%)
  Pallas kernels  8.81 us (7%)
  other arithmetic  5.56 us (5%)
  between operations  1.51 us (1%)
    all_gather x1, blocking collectives, local(): all_sums = lax.all_gather(totals, ('y', 'core'), axis=0, tiled=True)  28.8 us
    all_gather x1, blocking collectives, local(): right_class = lax.all_gather(right_root[0], 'q', axis=0, tiled=True)  18.9 us
    all_to_all x3, starting transfers between devices, exchange(): return lax.all_to_all(value, axes, 0, 0, tiled=True)  15.1 us
    all_gather x1, blocking collectives, local(): right_all = lax.all_gather(right_side, 'q', axis=0, tiled=True)  12.5 us
    all_to_all x1, blocking collectives, exchange(): return lax.all_to_all(value, axes, 0, 0, tiled=True)  11.3 us
    all_gather x1, blocking collectives, local(): totals = lax.all_gather(near_sums, 'q', axis=0, tiled=True)  8.41 us
    ppermute x2, starting transfers between devices, shifted(): lax.ppermute(value, axis, [(i, (i + by) % count) for i in range(count)])  6.88 us
    pallas_call x2, Pallas kernels, place(): pl.pallas_call(functools.partial(place_kernel, blocks), out_shape=jax.Sha...  3.44 us
  transfers between devices with their start and end apart: 6, of which 1 were waited for; matrix products, arithmetic and copies ran while one was open for 5% of the time, Pallas kernels for 1%

profile of v6, /device:TPU:1, one launch (start us, length us, event | category | flops | bytes accessed | tf_op | source)
XLA Modules:
  0.0 121.6 jit_solution(12900678644728834456)
XLA Ops:
  0.6 0.0 copy-start.2
  0.6 0.0 copy-start.3
  0.7 0.0 copy-start.4
  0.7 2.4 %pick.1 = f32[32,1024]{1,0:T(8,128)} custom-call(s32[16]{0:T(128)} %table.5, f32[32,16384]{1,0:T(8,128)} %gradient.1), custom_call_target="tpu_custom_call" | custom-call | tf_op jit(solution)/shard_map/pick/pallas_call | solution.py:44
  3.1 0.0 copy-start.1
  3.1 5.0 %collective-permute-start = (f32[32,1024]{1,0:T(8,128)}, f32[32,1024]{1,0:T(8,128)S(1)}, u32[]{:S(2)}, u32[]{:S(2)}) collective-permute-start(f32[32,1024]{1,0:T(8,128)} %pick.1), channel_id=1, source_target_pairs={{0,64},{64,0},{1,65},{65,1},{2,66},{66,2},{3,67},{67,3},{4,68},{68... | collective-permute-start | bytes 393224 | tf_op jit(solution)/shard_map/ppermute | solution.py:24
  8.0 0.0 copy-done.2
  8.0 1.9 %collective-permute-start.1 = (f32[32,1024]{1,0:T(8,128)S(1)}, f32[32,1024]{1,0:T(8,128)S(1)}, u32[]{:S(2)}, u32[]{:S(2)}) collective-permute-start(f32[32,1024]{1,0:T(8,128)S(1)} %bitcast.33), channel_id=1, source_target_pairs={{0,64},{64,0},{1,65},{65,1},{2,66},{66,2},{3,67},{67,3},{4,68},{68... | collective-permute-start | bytes 393224 | tf_op jit(solution)/shard_map/ppermute | solution.py:24
  10.7 0.0 copy-done.3
  10.7 0.0 copy-done.4
  10.7 2.3 %fusion.2 = (f32[1,32,1024]{2,1,0:T(8,128)}, f32[]{:T(128)}, f32[1,32,1024]{2,1,0:T(8,128)}) fusion(f32[32,1024]{1,0:T(8,128)} %pick.1, f32[1,32,1024]{2,1,0:T(8,128)S(1)} %copy-done.3, f32[]{:T(128)} %bitcast.4, f32[]{:T(128)} %bitcast.2, f32[1,32,1024]{2,1,0:T(8,128)S(1)} %copy-done.4), kind=kLoop, calls=%fused_computation.7 | loop fusion | flops 425983 | bytes 655372 | tf_op jit(solution)/shard_map/broadcast_in_dim | solution.py:210
  13.0 0.0 collective-permute-done
  13.0 2.1 %broadcast_select_fusion.1 = f32[4,2,32,1024]{3,2,1,0:T(8,128)} fusion(f32[32,1024]{1,0:T(8,128)S(1)} %collective-permute-done, f32[32,1024]{1,0:T(8,128)} %pick.1, pred[2]{0:T(512)(128)(4,1)S(1)} %iota_compare_fusion), kind=kLoop, calls=%fused_computation.1 | loop fusion | flops 262144 | bytes 1310722 | tf_op jit(solution)/shard_map/jit(_where)/select_n | solution.py:168
  15.1 0.0 collective-permute-done.1
  15.1 4.0 %all-to-all-start = ((f32[4,2,32,1024]{3,2,1,0:T(8,128)}), f32[4,2,32,1024]{3,2,1,0:T(8,128)S(1)}, u32[]{:S(2)}, u32[]{:S(2)}) async-start(f32[4,2,32,1024]{3,2,1,0:T(8,128)} %broadcast_select_fusion.1), calls=%async_computation | async-start | bytes 2097152 | tf_op jit(solution)/shard_map/all_to_all | solution.py:19
  19.1 0.0 copy-done.1
  19.1 18.9 %all-gather = f32[1,128,1024]{2,1,0:T(8,128)S(1)} all-gather(f32[1,32,1024]{2,1,0:T(8,128)S(1)} %copy-done.1), channel_id=2, replica_groups=mesh['q'=4,'r'=2,'x'=4,'y'=8,'core'=2] {'q'}, dimensions={1}, use_global_device_ids=true | all-gather | bytes 655360 | tf_op jit(solution)/shard_map/all_gather | solution.py:176
  38.0 1.1 broadcast_select_fusion
  39.2 0.0 all-to-all-done
  39.2 0.1 copy.14
  39.3 4.3 %all-to-all-start.1 = ((f32[4,2,32,1024]{3,2,1,0:T(8,128)}), f32[4,2,32,1024]{3,2,1,0:T(8,128)S(1)}, u32[]{:S(2)}, u32[]{:S(2)}) async-start(f32[4,2,32,1024]{3,2,1,0:T(8,128)} %broadcast_select_fusion), calls=%async_computation.1 | async-start | bytes 2097152 | tf_op jit(solution)/shard_map/all_to_all | solution.py:19
  43.5 1.0 fusion.3
  44.5 12.5 %all_gather.13.right = f32[1024,128]{1,0:T(8,128)S(1)} all-gather(f32[256,128]{1,0:T(8,128)S(1)} %fusion.3), channel_id=1, replica_groups=mesh['q'=4,'r'=2,'x'=4,'y'=8,'core'=2] {'q'}, dimensions={0}, use_global_device_ids=true | all-gather | bytes 655360 | tf_op jit(solution)/shard_map/all_gather | solution.py:198
  57.0 0.0 all-to-all-done.1.left
  57.0 1.8 %left_multiply.1 = f32[8,40,128]{2,1,0:T(8,128)S(1)} custom-call(f32[4,2,32,1024]{3,2,1,0:T(8,128)S(1)} %all-to-all-done.1.left, f32[1024,128]{1,0:T(8,128)S(1)} %all_gather.13.right, f32[1,1]{1,0:T(1,128)} %bitcast.8.adam), custom_call_target="tpu_custom_call" | custom-call | tf_op jit(solution)/shard_map/left_multiply/pallas_call | solution.py:75
  58.8 0.0 copy-start
  58.8 11.3 %all_to_all.20.held = f32[8,40,128]{2,1,0:T(8,128)S(1)} all-to-all(f32[8,40,128]{2,1,0:T(8,128)S(1)} %left_multiply.1), channel_id=1, replica_groups=mesh['q'=4,'r'=2,'x'=4,'y'=8,'core'=2] {'r','x'}, dimensions={0} | all-to-all | bytes 327680 | tf_op jit(solution)/shard_map/all_to_all | solution.py:19
  70.1 1.2 order_copies.1
  71.3 6.8 %all-to-all-start.3 = ((f32[8,32,1024]{2,1,0:T(8,128)}), f32[8,32,1024]{2,1,0:T(8,128)S(1)}, u32[]{:S(2)}, u32[]{:S(2)}) async-start(f32[8,32,1024]{2,1,0:T(8,128)} %order_copies.1), calls=%async_computation.3 | async-start | bytes 2097152 | tf_op jit(solution)/shard_map/all_to_all | solution.py:19
  78.1 8.4 %all-gather.3 = f32[4,1,128]{2,1,0:T(1,128)S(1)} all-gather(f32[1,1,128]{2,1,0:T(1,128)S(1)} %bitcast.35), channel_id=3, replica_groups=mesh['q'=4,'r'=2,'x'=4,'y'=8,'core'=2] {'q'}, dimensions={0}, use_global_device_ids=true | all-gather | bytes 2560 | tf_op jit(solution)/shard_map/all_gather | solution.py:202
  86.6 28.8 %all-gather.4 = f32[16,1,128]{2,1,0:T(1,128)S(1)} all-gather(f32[1,1,128]{2,1,0:T(1,128)S(1)} %bitcast.36), channel_id=4, replica_groups=mesh['q'=4,'r'=2,'x'=4,'y'=8,'core'=2] {'y','core'}, dimensions={0}, use_global_device_ids=true | all-gather | bytes 8704 | tf_op jit(solution)/shard_map/all_gather | solution.py:205
  115.4 0.0 all-to-all-done.3.held
  115.4 2.1 %collective-permute-start.2 = (f32[8,32,1024]{2,1,0:T(8,128)S(1)}, f32[8,32,1024]{2,1,0:T(8,128)S(1)}, u32[]{:S(2)}, u32[]{:S(2)}) collective-permute-start(f32[8,32,1024]{2,1,0:T(8,128)S(1)} %all-to-all-done.3.held), channel_id=1, source_target_pairs={{0,1},{1,0},{2,3},{3,2},{4,5},{5,4},{6,7},{7,6},{8,9},{9,8},{10,11... | collective-permute-start | bytes 3145736 | tf_op jit(solution)/shard_map/ppermute | solution.py:207
  117.5 0.0 copy-done
  117.5 1.7 %place_own.1.rest_0_ = f32[32,16384]{1,0:T(8,128)} custom-call(s32[16]{0:T(128)S(1)} %copy-done, f32[16,128]{1,0:T(8,128)S(1)} %bitcast.28, f32[8,32,1024]{2,1,0:T(8,128)S(1)} %all-to-all-done.3.held), custom_call_target="tpu_custom_call" | custom-call | bytes 2097152 | tf_op jit(solution)/shard_map/place_own/pallas_call | solution.py:137
  119.3 0.7 collective-permute-done.2.held
  119.9 1.7 %place_other.1 = f32[32,16384]{1,0:T(8,128)} custom-call(s32[16]{0:T(128)S(1)} %copy-done, f32[16,128]{1,0:T(8,128)S(1)} %bitcast.29, f32[8,32,1024]{2,1,0:T(8,128)S(1)} %collective-permute-done.2.held, f32[32,16384]{1,0:T(8,128)} %place_own.1.rest_0_), custom_call_target="tpu_custom_call", output_to_operand_aliasing={{}: (3, {})} | custom-call | bytes 2097152 | tf_op jit(solution)/shard_map/place_other/pallas_call | solution.py:137
  (3 shorter events, 0.1 us)
Async XLA Ops:
  0.6 7.4 %copy-start.2 = (f32[1,32,1024]{2,1,0:T(8,128)S(1)}, f32[1,32,1024]{2,1,0:T(8,128)}, u32[]{:S(2)}) copy-start(f32[1,32,1024]{2,1,0:T(8,128)} %param.8) | copy-start | bytes 393220
  0.6 10.1 %copy-start.3 = (f32[1,32,1024]{2,1,0:T(8,128)S(1)}, f32[1,32,1024]{2,1,0:T(8,128)}, u32[]{:S(2)}) copy-start(f32[1,32,1024]{2,1,0:T(8,128)} %param.11) | copy-start | bytes 393220
  0.7 10.1 %copy-start.4 = (f32[1,32,1024]{2,1,0:T(8,128)S(1)}, f32[1,32,1024]{2,1,0:T(8,128)}, u32[]{:S(2)}) copy-start(f32[1,32,1024]{2,1,0:T(8,128)} %param.10) | copy-start | bytes 393220
  3.1 16.1 %copy-start.1 = (f32[1,32,1024]{2,1,0:T(8,128)S(1)}, f32[1,32,1024]{2,1,0:T(8,128)}, u32[]{:S(2)}) copy-start(f32[1,32,1024]{2,1,0:T(8,128)} %param.9) | copy-start | bytes 393220
  3.1 10.0 %collective-permute-start = (f32[32,1024]{1,0:T(8,128)}, f32[32,1024]{1,0:T(8,128)S(1)}, u32[]{:S(2)}, u32[]{:S(2)}) collective-permute-start(f32[32,1024]{1,0:T(8,128)} %pick.1), channel_id=1, source_target_pairs={{0,64},{64,0},{1,65},{65,1},{2,66},{66,2},{3,67},{67,3},{4,68},{68... | collective-permute-start | bytes 393224 | tf_op jit(solution)/shard_map/ppermute | solution.py:24
  8.0 7.1 %collective-permute-start.1 = (f32[32,1024]{1,0:T(8,128)S(1)}, f32[32,1024]{1,0:T(8,128)S(1)}, u32[]{:S(2)}, u32[]{:S(2)}) collective-permute-start(f32[32,1024]{1,0:T(8,128)S(1)} %bitcast.33), channel_id=1, source_target_pairs={{0,64},{64,0},{1,65},{65,1},{2,66},{66,2},{3,67},{67,3},{4,68},{68... | collective-permute-start | bytes 393224 | tf_op jit(solution)/shard_map/ppermute | solution.py:24
  15.1 24.1 %all-to-all-start = ((f32[4,2,32,1024]{3,2,1,0:T(8,128)}), f32[4,2,32,1024]{3,2,1,0:T(8,128)S(1)}, u32[]{:S(2)}, u32[]{:S(2)}) async-start(f32[4,2,32,1024]{3,2,1,0:T(8,128)} %broadcast_select_fusion.1), calls=%async_computation | async-start | bytes 2097152 | tf_op jit(solution)/shard_map/all_to_all | solution.py:19
  39.3 17.7 %all-to-all-start.1 = ((f32[4,2,32,1024]{3,2,1,0:T(8,128)}), f32[4,2,32,1024]{3,2,1,0:T(8,128)S(1)}, u32[]{:S(2)}, u32[]{:S(2)}) async-start(f32[4,2,32,1024]{3,2,1,0:T(8,128)} %broadcast_select_fusion), calls=%async_computation.1 | async-start | bytes 2097152 | tf_op jit(solution)/shard_map/all_to_all | solution.py:19
  58.8 58.7 %copy-start = (s32[16]{0:T(128)S(1)}, s32[16]{0:T(128)}, u32[]{:S(2)}) copy-start(s32[16]{0:T(128)} %table.5) | copy-start | bytes 196
  71.3 44.1 %all-to-all-start.3 = ((f32[8,32,1024]{2,1,0:T(8,128)}), f32[8,32,1024]{2,1,0:T(8,128)S(1)}, u32[]{:S(2)}, u32[]{:S(2)}) async-start(f32[8,32,1024]{2,1,0:T(8,128)} %order_copies.1), calls=%async_computation.3 | async-start | bytes 2097152 | tf_op jit(solution)/shard_map/all_to_all | solution.py:19
  115.4 4.5 %collective-permute-start.2 = (f32[8,32,1024]{2,1,0:T(8,128)S(1)}, f32[8,32,1024]{2,1,0:T(8,128)S(1)}, u32[]{:S(2)}, u32[]{:S(2)}) collective-permute-start(f32[8,32,1024]{2,1,0:T(8,128)S(1)} %all-to-all-done.3.held), channel_id=1, source_target_pairs={{0,1},{1,0},{2,3},{3,2},{4,5},{5,4},{6,7},{7,6},{8,9},{9,8},{10,11... | collective-permute-start | bytes 3145736 | tf_op jit(solution)/shard_map/ppermute | solution.py:207
